TPU v7x, 32 devices: a whole 2x2x4 slice. The times are simulated.
32 devices in a mesh: rep: 2 (over y), tm: 4 (over z), tk: 4 (over x, core).
Axes of the slice: x: 2, y: 2, z: 4, core: 2. Of those that a mesh axis runs over, the one named last changes fastest.
Arguments:
- hidden_in: bfloat16 [2, 128, 8192], P(None, ('rep', 'tm'), 'tk'), parts along dimension 1, may hold values from -6 to 6
- gate_weight: bfloat16 [8192, 28672], P('tk', 'tm'), may hold values from -0.0625 to 0.0625
- up_weight: bfloat16 [8192, 28672], P('tk', 'tm'), may hold values from -0.0625 to 0.0625
- shrink_store: bfloat16 [4, 8192, 128], P('tm', 'tk'), may hold values from -0.0625 to 0.0625
- expand_gate: bfloat16 [4, 64, 28672], P('tk', None, 'tm'), may hold values from -0.75 to 0.75
- expand_up: bfloat16 [4, 64, 28672], P('tk', None, 'tm'), may hold values from -0.75 to 0.75
- block_adapter: int32 [2, 16], P(None, 'rep'), parts along dimension 1, may hold values from 0 to 3
- store_slot: int32 [4], replicated, may hold values from 0 to 3, each once
Outputs:
- activated: bfloat16 [128, 2, 28672], P(('rep', 'tk'), None, 'tm'), parts along dimension 0
There are 2 independent parts, one for each index of `rep`. A program takes and returns all parts, laid end to end along the dimension named above; an argument that names none is the same for every part. Nothing has to cross between parts.
Inputs may be any that keep to these rules, and one draw needn't show every extreme that they name: store_slot names every store position once; position p lies with index p // 1 of tm.
All inputs are finite; a program needn't handle non-finite values.
Results may differ from a plain program's by a relative error of at most 0.0049.
Values may be sent and summed in bfloat16 or wider, within the bound.
No kernel may reach another device: no remote copies, remote signals or barrier semaphores. Data moves between devices by JAX's collectives and lax.ppermute only.
A program may use at most 192 MiB of HBM per device.

v0:
```python
import jax
import jax.numpy as jnp
from jax import lax
from jax.sharding import PartitionSpec as P

BLOCK = 8


def slots_of_rows(block_adapter, store_slot):
    count = store_slot.shape[0]
    match = block_adapter[:, :, None] == jnp.arange(count, dtype=jnp.int32)
    block_slot = jnp.sum(jnp.where(match, store_slot, 0), axis=2)
    return jnp.repeat(block_slot, BLOCK, axis=1)


def shrink_part(gathered, row_slot, shrink_store):
    owned = shrink_store.shape[0]
    first = lax.axis_index("tm") * owned
    product = jnp.einsum(
        "srd,adk->srak", gathered, shrink_store, preferred_element_type=jnp.float32
    )
    chosen = row_slot[:, :, None] == first + jnp.arange(owned, dtype=jnp.int32)
    return jnp.sum(jnp.where(chosen[..., None], product, 0.0), axis=2)


def spread_ranks(row_ranks, row_slots, held_first, held, rank, which):
    piece = row_ranks[:, :, which * rank : (which + 1) * rank]
    chosen = row_slots[:, :, None] == held_first + jnp.arange(held, dtype=jnp.int32)
    spread = jnp.where(chosen[..., None], piece[:, :, None, :], jnp.zeros((), jnp.bfloat16))
    return spread.reshape(piece.shape[0], piece.shape[1], held * rank)


def make_term(gathered, shrunk, row_slot, gate_weight, up_weight, expand_gate, expand_up):
    held = expand_gate.shape[0]
    rank = expand_gate.shape[1]
    width = expand_gate.shape[2]
    held_first = lax.axis_index("tk") * held
    stack_gate = expand_gate.reshape(held * rank, width)
    stack_up = expand_up.reshape(held * rank, width)

    def term(start, count):
        gate_sum = jnp.einsum(
            "scd,df->csf", gathered, gate_weight, preferred_element_type=jnp.float32
        )
        gate_sum = gate_sum + jnp.einsum(
            "sch,hf->csf",
            spread_ranks(shrunk, row_slot, held_first, held, rank, 0),
            stack_gate,
            preferred_element_type=jnp.float32,
        )
        up_sum = jnp.einsum("scd,df->csf", gathered, up_weight, preferred_element_type=jnp.float32)
        up_sum = up_sum + jnp.einsum(
            "sch,hf->csf",
            spread_ranks(shrunk, row_slot, held_first, held, rank, 1),
            stack_up,
            preferred_element_type=jnp.float32,
        )
        joined = jnp.concatenate([gate_sum, up_sum], axis=2)
        return joined.reshape(count, -1)

    return term


def finish(summed, steps_here, width):
    pieces = summed.reshape(summed.shape[0], steps_here, 2, width)
    return (jax.nn.silu(pieces[:, :, 0, :]) * pieces[:, :, 1, :]).astype(jnp.bfloat16)


def on_device(
    hidden_in,
    gate_weight,
    up_weight,
    shrink_store,
    expand_gate,
    expand_up,
    block_adapter,
    store_slot,
):
    row_slot = slots_of_rows(block_adapter, store_slot)
    width = gate_weight.shape[1]
    members = lax.axis_size("tk")
    gathered = lax.all_gather(hidden_in, "tm", axis=1, tiled=True)
    shrunk = lax.psum(shrink_part(gathered, row_slot, shrink_store), ("tm", "tk")).astype(
        jnp.bfloat16
    )
    term = make_term(gathered, shrunk, row_slot, gate_weight, up_weight, expand_gate, expand_up)
    summed = lax.psum_scatter(
        term(jnp.int32(0), gathered.shape[1] // members * lax.axis_size("tk")),
        "tk",
        scatter_dimension=0,
        tiled=True,
    )
    return finish(summed, gathered.shape[0], width)


def solution(mesh):
    return jax.shard_map(
        on_device,
        mesh=mesh,
        in_specs=(
            P(None, ("rep", "tm"), "tk"),
            P("tk", "tm"),
            P("tk", "tm"),
            P("tm", "tk", None),
            P("tk", None, "tm"),
            P("tk", None, "tm"),
            P(None, "rep"),
            P(),
        ),
        out_specs=P(("rep", "tk"), None, "tm"),
        check_vma=False,
    )
```

profile of v0, /device:TPU:0, one launch (start us, length us, event | category | flops | bytes accessed | tf_op | source)
XLA Modules:
  0.0 195.2 jit_solution(4798116983761068349)
XLA Ops:
  6.5 0.0 copy-start
  6.5 0.0 reduce-scatter.2.cloned.1.call-start
  6.5 0.9 select_reduce_fusion
  7.4 0.1 broadcast_in_dim.50
  7.5 0.1 eq.58
  7.6 0.1 broadcast_in_dim.52
  7.7 0.1 eq.61
  7.7 17.6 %all_gather.3 = bf16[2,64,2048]{2,1,0:T(8,128)(2,1)S(1)} all-gather(bf16[2,16,2048]{2,1,0:T(8,128)(2,1)} %param.8), channel_id=1, replica_groups=mesh['rep'=2,'tm'=4,'tk'=4] {'tm'}, dimensions={1}, use_global_device_ids=true | all-gather | bytes 655360 | tf_op jit(solution)/shard_map/all_gather | solution.py:82
  25.3 1.3 convolution_select_fusion
  26.6 58.4 %psum.7 = bf16[2,64,128]{2,1,0:T(8,128)(2,1)S(1)} all-reduce(f32[2,64,128]{2,1,0:T(8,128)S(1)} %convolution_select_fusion), channel_id=1, replica_groups=mesh['rep'=2,'tm'=4,'tk'=4] {'tm','tk'}, use_global_device_ids=true, to_apply=%region_1.2 | all-reduce | flops 16384 | bytes 98304 | tf_op jit(solution)/shard_map/psum | solution.py:83
  85.1 11.6 %fusion.7 = f32[64,2,7168]{2,0,1:T(8,128)S(1)} fusion(bf16[2,64,2048]{2,1,0:T(8,128)(2,1)S(1)} %all_gather.3, bf16[2048,7168]{1,0:T(8,128)(2,1)} %param.10), kind=kOutput, calls=%fused_computation.5 | convolution fusion | flops 3758096384 | bytes 33554432 | tf_op jit(solution)/shard_map/scd,df->csf/dot_general | solution.py:51
  96.7 15.3 %fusion.4 = f32[64,2,7168]{2,0,1:T(8,128)} fusion(bf16[2,64,2048]{2,1,0:T(8,128)(2,1)S(1)} %all_gather.3, bf16[2048,7168]{1,0:T(8,128)(2,1)} %param.9), kind=kOutput, calls=%fused_computation.4 | convolution fusion | flops 3758096384 | bytes 33554432 | tf_op jit(solution)/shard_map/scd,df->csf/dot_general | solution.py:42
  112.0 0.0 copy-done
  112.0 0.0 copy-start.1
  112.0 0.0 copy-start.2
  112.0 0.7 fusion.10
  112.7 1.3 copy-done.1
  114.0 0.2 copy-done.2
  114.3 0.7 fusion.11
  115.0 0.7 maximum_bitcast_fusion
  115.7 3.5 %copy.15 = f32[2,8,8,14336]{3,2,0,1:T(8,128)} copy(f32[2,8,8,14336]{3,2,1,0:T(8,128)S(1)} %maximum_bitcast_fusion) | data formatting | bytes 14680064 | tf_op jit(solution)/shard_map/reshape | solution.py:59
  119.1 0.0 reduce-scatter.2.cloned.1.call-update
  119.2 62.9 %reduce-scatter.2.cloned.1.call-done = f32[16,28672]{1,0:T(8,128)} async-done(((f32[64,28672]{1,0:T(8,128)}), f32[16,28672]{1,0:T(8,128)}) %reduce-scatter.2.cloned.1.call-update) | async-done | bytes 1835024 | tf_op jit(solution)/shard_map/reduce_scatter | solution.py:87
  182.1 3.1 %reshape.60 = f32[16,2,2,7168]{3,2,1,0:T(2,128)S(1)} reshape(f32[16,28672]{1,0:T(8,128)} %reduce-scatter.2.cloned.1.call-done) | data formatting | bytes 3670016 | tf_op jit(solution)/shard_map/reshape | solution.py:65
  185.1 1.4 fusion.23
  186.6 1.8 fusion.15
  (1 shorter events, 0.0 us)
Async XLA Ops:
  6.5 105.5 %copy-start = (bf16[1,64,7168]{2,1,0:T(8,128)(2,1)S(1)}, bf16[1,64,7168]{2,1,0:T(8,128)(2,1)}, u32[]{:S(2)}) copy-start(bf16[1,64,7168]{2,1,0:T(8,128)(2,1)} %param.13) | copy-start | bytes 2752516
  6.5 175.5 %reduce-scatter.2.cloned.1.call-start = ((), (), s32[]{:S(2)}) async-start(), calls=%async_computation.1 | async-start | bytes 9175040 | tf_op jit(solution)/shard_map/reduce_scatter | solution.py:87
  112.0 2.0 %copy-start.1 = (f32[64,2,7168]{2,0,1:T(8,128)S(1)}, f32[64,2,7168]{2,0,1:T(8,128)}, u32[]{:S(2)}) copy-start(f32[64,2,7168]{2,0,1:T(8,128)} %fusion.4) | copy-start | bytes 11010052
  112.0 2.3 %copy-start.2 = (bf16[1,64,7168]{2,1,0:T(8,128)(2,1)S(1)}, bf16[1,64,7168]{2,1,0:T(8,128)(2,1)}, u32[]{:S(2)}) copy-start(bf16[1,64,7168]{2,1,0:T(8,128)(2,1)} %param.12) | copy-start | bytes 2752516
Sparse Core Ops, SparseCore 0:
  119.3 62.7 reduce-scatter.1
where the time goes:
time: 195 us
  blocking collectives  76 us (39%)
  waiting for transfers between devices  62.9 us (32%)
  matrix products  29.6 us (15%)
  between operations  13.4 us (7%)
  local copies, waits for them, and re-layouts  9.88 us (5%)
  other arithmetic  3.3 us (2%)
    reduce_scatter x1, waiting for transfers between devices, on_device(): lax.psum_scatter(term(jnp.int32(0), gathered.shape[1] // members * lax.ax...  62.9 us
    psum x1, blocking collectives, on_device(): lax.psum(shrink_part(gathered, row_slot, shrink_store), ('tm', 'tk'))  58.4 us
    all_gather x1, blocking collectives, on_device(): gathered = lax.all_gather(hidden_in, 'tm', axis=1, tiled=True)  17.6 us
    dot_general x1, matrix products, term(): jnp.einsum('scd,df->csf', gathered, gate_weight, preferred_element_type=j...  15.3 us
    dot_general x1, matrix products, term(): jnp.einsum('scd,df->csf', gathered, up_weight, preferred_element_type=jnp...  11.6 us
  transfers between devices with their start and end apart: 1, of which 1 were waited for; matrix products, arithmetic and copies ran while one was open for 0% of the time, Pallas kernels for 0%

commit v1 on v0

v1 whole, which is shorter than its diff:
```python
import functools

import jax
import jax.numpy as jnp
from jax import lax
from jax.experimental import pallas as pl
from jax.experimental.pallas import tpu as pltpu
from jax.sharding import PartitionSpec as P

BLOCK = 8
MIB = 2**20
F32 = jnp.float32
BF16 = jnp.bfloat16
CHUNKS = (1024, 2048, 2048, 2048)
TILE = 256


def slots_of_rows(block_adapter, store_slot):
    count = store_slot.shape[0]
    match = block_adapter[:, :, None] == jnp.arange(count, dtype=jnp.int32)
    block_slot = jnp.sum(jnp.where(match, store_slot, 0), axis=2)
    return jnp.repeat(block_slot, BLOCK, axis=1)


def shrink_part(gathered, row_slot, shrink_store):
    owned = shrink_store.shape[0]
    first = lax.axis_index("tm") * owned
    product = jnp.einsum(
        "srd,adk->srak", gathered, shrink_store, preferred_element_type=F32
    )
    chosen = row_slot[:, :, None] == first + jnp.arange(owned, dtype=jnp.int32)
    return jnp.sum(jnp.where(chosen[..., None], product, 0.0), axis=2)


def spread_ranks(row_ranks, row_slots, held_first, held, rank, which):
    piece = row_ranks[:, :, which * rank : (which + 1) * rank]
    chosen = row_slots[:, :, None] == held_first + jnp.arange(held, dtype=jnp.int32)
    spread = jnp.where(chosen[..., None], piece[:, :, None, :], jnp.zeros((), BF16))
    return spread.reshape(piece.shape[0], piece.shape[1], held * rank)


def make_term(gathered, shrunk, row_slot, gate_weight, up_weight, expand_gate, expand_up):
    held = expand_gate.shape[0]
    rank = expand_gate.shape[1]
    width = expand_gate.shape[2]
    held_first = lax.axis_index("tk") * held
    stack_gate = expand_gate.reshape(held * rank, width)
    stack_up = expand_up.reshape(held * rank, width)

    def one(weight, stack, which):
        total = jnp.einsum("scd,df->csf", gathered, weight, preferred_element_type=F32)
        return total + jnp.einsum(
            "sch,hf->csf",
            spread_ranks(shrunk, row_slot, held_first, held, rank, which),
            stack,
            preferred_element_type=F32,
        )

    joined = jnp.concatenate(
        [one(gate_weight, stack_gate, 0), one(up_weight, stack_up, 1)], axis=2
    )
    return joined.reshape(gathered.shape[1], -1)


def on_any_mesh(
    hidden_in,
    gate_weight,
    up_weight,
    shrink_store,
    expand_gate,
    expand_up,
    block_adapter,
    store_slot,
):
    row_slot = slots_of_rows(block_adapter, store_slot)
    width = gate_weight.shape[1]
    gathered = lax.all_gather(hidden_in, "tm", axis=1, tiled=True)
    shrunk = lax.psum(
        shrink_part(gathered, row_slot, shrink_store), ("tm", "tk")
    ).astype(BF16)
    term = make_term(
        gathered, shrunk, row_slot, gate_weight, up_weight, expand_gate, expand_up
    )
    summed = lax.psum_scatter(term, "tk", scatter_dimension=0, tiled=True)
    pieces = summed.reshape(summed.shape[0], gathered.shape[0], 2, width)
    return (jax.nn.silu(pieces[:, :, 0, :]) * pieces[:, :, 1, :]).astype(BF16)


def swap_bits(value):
    return ((value & 1) << 1) | (value >> 1)


def block_slots(adapter_ref, slot_ref, group, steps, blocks):
    return [
        slot_ref[adapter_ref[step, group * blocks + block]]
        for step in range(steps)
        for block in range(blocks)
    ]


def assemble_kernel(own, one, two, three, shrink, rows_out, part_out):
    z = lax.axis_index("tm")
    t = lax.axis_index("tk")
    size = own.shape[0]
    for k, piece in enumerate((own, one, two, three)):
        place = swap_bits(z ^ t ^ k)
        rows_out[pl.ds(pl.multiple_of(place * size, size), size), :] = piece[...]
    part = jnp.dot(rows_out[...], shrink[...], preferred_element_type=F32)
    for place in range(4):
        group = t ^ swap_bits(place)
        part_out[pl.ds(pl.multiple_of(group * size, size), size), :] = part[
            place * size : (place + 1) * size
        ]


def assemble(pieces, shrink):
    rows = 4 * pieces[0].shape[0]
    depth, ranks = shrink.shape
    vmem = pl.BlockSpec(memory_space=pltpu.VMEM)
    return pl.pallas_call(
        assemble_kernel,
        in_specs=[vmem] * 5,
        out_specs=[vmem] * 2,
        out_shape=[
            jax.ShapeDtypeStruct((rows, depth), BF16),
            jax.ShapeDtypeStruct((rows, ranks), F32),
        ],
        compiler_params=pltpu.CompilerParams(vmem_limit_bytes=8 * MIB),
        cost_estimate=pl.CostEstimate(
            flops=2 * rows * depth * ranks, bytes_accessed=2 * MIB, transcendentals=0
        ),
        name="assemble_and_shrink",
    )(*pieces, shrink)


def spread_kernel(blocks, adapter_ref, slot_ref, first, second, out):
    t = lax.axis_index("tk")
    steps = adapter_ref.shape[0]
    size = first.shape[0] // 4
    parts = []
    for place in range(4):
        group = t ^ swap_bits(place)
        rows = pl.ds(pl.multiple_of(group * size, size), size)
        total = first[rows, :] + second[rows, :]
        slots = block_slots(adapter_ref, slot_ref, group, steps, blocks)
        for i, slot in enumerate(slots):
            here = total[i * BLOCK : (i + 1) * BLOCK]
            parts.append(jnp.where(slot == t, here, jnp.zeros_like(here)))
    out[...] = jnp.concatenate(parts, axis=0).astype(BF16)


def spread(first, second, block_adapter, store_slot):
    rows, ranks = first.shape
    blocks = block_adapter.shape[1] // 4
    vmem = pl.BlockSpec(memory_space=pltpu.VMEM)
    smem = pl.BlockSpec(memory_space=pltpu.SMEM)
    return pl.pallas_call(
        functools.partial(spread_kernel, blocks),
        in_specs=[smem, smem, vmem, vmem],
        out_specs=vmem,
        out_shape=jax.ShapeDtypeStruct((rows, ranks), BF16),
        compiler_params=pltpu.CompilerParams(vmem_limit_bytes=4 * MIB),
        cost_estimate=pl.CostEstimate(
            flops=2 * rows * ranks, bytes_accessed=rows * ranks * 10, transcendentals=0
        ),
        name="spread",
    )(block_adapter, store_slot, first, second)


def load_kernel(plan, *refs):
    sem = refs[-1]
    sources, targets = refs[: -1 - len(plan)], refs[-1 - len(plan) : -1]
    copies = []
    for i, (which, start, cols) in enumerate(plan):
        source = sources[which]
        source = source.at[0] if start is None else source.at[:, pl.ds(start, cols)]
        copies.append(pltpu.make_async_copy(source, targets[i], sem.at[i]))
    for copy in copies:
        copy.start()
    for copy in copies:
        copy.wait()


def load(plan, *arrays):
    shapes = [
        arrays[which].shape[1:] if start is None else (arrays[which].shape[0], cols)
        for which, start, cols in plan
    ]
    size = sum(2 * a * b for a, b in shapes)
    return pl.pallas_call(
        functools.partial(load_kernel, plan),
        in_specs=[pl.BlockSpec(memory_space=pltpu.HBM)] * len(arrays),
        out_specs=[pl.BlockSpec(memory_space=pltpu.VMEM)] * len(plan),
        out_shape=[pltpu.VMEM(shape, BF16) for shape in shapes],
        scratch_shapes=[pltpu.SemaphoreType.DMA((len(plan),))],
        compiler_params=pltpu.CompilerParams(vmem_limit_bytes=2 * MIB),
        cost_estimate=pl.CostEstimate(flops=0, bytes_accessed=2 * size, transcendentals=0),
        name="load",
    )(*[far(a) for a in arrays])


def product_kernel(
    start, cols, fetch, tile, x_ref, ranks_ref, gate, up, eg, eu, send, keep, buffer, sem
):
    rank = ranks_ref.shape[1] // 2
    rows = x_ref.shape[0]
    half, quarter = rows // 2, rows // 4

    def copy(j):
        return pltpu.make_async_copy(
            up.at[:, pl.ds(start + j * fetch, fetch)],
            buffer.at[:, pl.ds(j * fetch, fetch)],
            sem.at[j],
        )

    for j in range(cols // fetch):
        copy(j).start()
    for which in range(2):
        base = which * quarter
        for j in range(cols // tile):
            at = slice(j * tile, (j + 1) * tile)
            there = slice(start + j * tile, start + (j + 1) * tile)
            if which == 0:
                weight = gate[:, at]
            else:
                if j * tile % fetch == 0:
                    copy(j * tile // fetch).wait()
                weight = buffer[:, at]
            y = jnp.dot(x_ref[...], weight, preferred_element_type=F32)
            y += jnp.dot(
                ranks_ref[:, which * rank : (which + 1) * rank],
                (eg, eu)[which][:, there],
                preferred_element_type=F32,
            )
            keep[base : base + quarter, at] = y[quarter:half]
            keep[half + base : half + base + quarter, at] = y[:quarter]
            send[base : base + quarter, at] = y[half + quarter :].astype(BF16)
            send[half + base : half + base + quarter, at] = y[half : half + quarter].astype(BF16)


def product(x, ranks, gate, up, eg, eu, start, cols):
    rows, depth = x.shape
    fetch = 512 if cols % 512 == 0 else cols // 2
    vmem = pl.BlockSpec(memory_space=pltpu.VMEM)
    hbm = pl.BlockSpec(memory_space=pltpu.HBM)
    return pl.pallas_call(
        functools.partial(product_kernel, start, cols, fetch, TILE),
        in_specs=[vmem, vmem, vmem, hbm, vmem, vmem],
        out_specs=[vmem, vmem],
        out_shape=[
            pltpu.VMEM((rows, cols), BF16),
            pltpu.VMEM((rows, cols), F32),
        ],
        scratch_shapes=[
            pltpu.VMEM((depth, cols), BF16),
            pltpu.SemaphoreType.DMA((cols // fetch,)),
        ],
        compiler_params=pltpu.CompilerParams(vmem_limit_bytes=12 * MIB),
        cost_estimate=pl.CostEstimate(
            flops=4 * rows * depth * cols, bytes_accessed=4 * depth * cols, transcendentals=0
        ),
        name="product",
    )(x, ranks, near(gate), far(up), near(eg), near(eu))


def near(value):
    return pltpu.with_memory_space_constraint(value, pltpu.VMEM)


def far(value):
    return pltpu.with_memory_space_constraint(value, pltpu.HBM)


def on_pairs(
    hidden_in,
    gate_weight,
    up_weight,
    shrink_store,
    expand_gate,
    expand_up,
    block_adapter,
    store_slot,
):
    steps, here, depth = hidden_in.shape
    own = hidden_in.reshape(steps * here, depth)
    rows = 4 * steps * here

    def exchange(value, axis, bit):
        return lax.ppermute(value, axis, [(i, i ^ bit) for i in range(4)])

    three = exchange(own, "tm", 3)
    two = exchange(own, "tm", 2)
    one = exchange(own, "tm", 1)
    plan = [(0, None, None), (1, None, None), (2, None, None)]
    start = 0
    for cols in CHUNKS:
        plan.append((3, start, cols))
        start += cols
    shrink, eg, eu, *gates = load(
        tuple(plan), shrink_store, expand_gate, expand_up, gate_weight
    )
    x, part = assemble((own, one, two, three), shrink)

    pair = part + exchange(part, "tk", 1)

    def deliver(j):
        perm = []
        for a in range(4):
            for t in range(4):
                chip, core = t >> 1, t & 1
                perm.append((a * 4 + t, (2 * core + (chip ^ j)) * 4 + a))
        return lax.ppermute(pair, ("tm", "tk"), perm)

    ranks = spread(deliver(0), deliver(1), block_adapter, store_slot)

    half, quarter = rows // 2, rows // 4
    outs = []
    start = 0
    overs = []
    for j, cols in enumerate(CHUNKS):
        if j > 0:
            x, _ = lax.optimization_barrier((x, overs[max(j - 2, 0)]))
        send, keep = product(x, ranks, gates[j], up_weight, eg, eu, start, cols)
        got = exchange(send, "tk", 1)
        over = (keep[:half] + got[:half]).astype(BF16)
        overs.append(over)
        other = exchange(over, "tk", 2)
        total = keep[half:] + got[half:] + other
        gate, up = total[:quarter], total[quarter:]
        outs.append((jax.nn.silu(gate) * up).astype(BF16))
        start += cols
    out = jnp.concatenate(outs, axis=1).reshape(steps, here, -1)
    return jnp.transpose(out, (1, 0, 2))


def solution(mesh):
    paired = mesh.shape["tm"] == 4 and mesh.shape["tk"] == 4
    return jax.shard_map(
        on_pairs if paired else on_any_mesh,
        mesh=mesh,
        in_specs=(
            P(None, ("rep", "tm"), "tk"),
            P("tk", "tm"),
            P("tk", "tm"),
            P("tm", "tk", None),
            P("tk", None, "tm"),
            P("tk", None, "tm"),
            P(None, "rep"),
            P(),
        ),
        out_specs=P(("rep", "tk"), None, "tm"),
        check_vma=False,
    )
```

time: 195 us -> 69 us (0.35)
  blocking collectives: 76 us -> 0 us
  waiting for transfers between devices: 62.9 us -> 20.2 us
  matrix products: 29.6 us -> 0 us
  Pallas kernels: 0 us -> 29.3 us
  starting transfers between devices: 0.01 us -> 17 us
  between operations: 13.4 us -> 0.2 us
  local copies, waits for them, and re-layouts: 9.88 us -> 1.25 us
  other arithmetic: 3.3 us -> 0.81 us
    reduce_scatter x1 -> x0, waiting for transfers between devices: 62.9 us -> none  [on_device(): lax.psum_scatter(term(jnp.int32(0), gathered.shape[1] // members * lax.ax...]
    psum x1 -> x0, blocking collectives: 58.4 us -> none  [on_device(): lax.psum(shrink_part(gathered, row_slot, shrink_store), ('tm', 'tk'))]
    dot_general x5 -> x0, matrix products: 29.6 us -> none  [the longest x1 15.3 us: term(): jnp.einsum('scd,df->csf', gathered, gate_weight, preferred_element_type=j...]
    pallas_call x0 -> x7, Pallas kernels: none -> 29.3 us  [the longest x4 18.1 us: product(): pl.pallas_call(functools.partial(product_kernel, start, cols, fetch, TILE...]
    ppermute x0 -> x14, waiting for transfers between devices: none -> 20.2 us  [the longest x12 17.6 us: exchange(): return lax.ppermute(value, axis, [(i, i ^ bit) for i in range(4)])]
    all_gather x1 -> x0, blocking collectives: 17.6 us -> none  [on_device(): gathered = lax.all_gather(hidden_in, 'tm', axis=1, tiled=True)]
    ppermute x0 -> x14, starting transfers between devices: none -> 17 us  [the longest x12 15.4 us: exchange(): return lax.ppermute(value, axis, [(i, i ^ bit) for i in range(4)])]
    reshape x2 -> x1, local copies, waits for them, and re-layouts: 6.53 us -> 1.24 us  [on_pairs(): out = jnp.concatenate(outs, axis=1).reshape(steps, here, -1)]
  transfers between devices with their start and end apart: 1 -> 14, of which waited for: 1 -> 8; matrix products, arithmetic and copies ran while one was open for 0% -> 1% of each run, Pallas kernels for 0% -> 37%
where the time goes in v1:
time: 69 us; the launch traced here: 68.8 us
  Pallas kernels  29.3 us (42%)
  waiting for transfers between devices  20.2 us (29%)
  starting transfers between devices  17 us (25%)
  local copies, waits for them, and re-layouts  1.25 us (2%)
  other arithmetic  0.81 us (1%)
    pallas_call x4, Pallas kernels, product(): pl.pallas_call(functools.partial(product_kernel, start, cols, fetch, TILE...  18.1 us
    ppermute x12, waiting for transfers between devices, exchange(): return lax.ppermute(value, axis, [(i, i ^ bit) for i in range(4)])  17.6 us
    ppermute x12, starting transfers between devices, exchange(): return lax.ppermute(value, axis, [(i, i ^ bit) for i in range(4)])  15.4 us
    pallas_call x1, Pallas kernels, load(): pl.pallas_call(functools.partial(load_kernel, plan), in_specs=[pl.BlockSp...  10.2 us
    ppermute x2, waiting for transfers between devices, deliver(): return lax.ppermute(pair, ('tm', 'tk'), perm)  2.64 us
    ppermute x2, starting transfers between devices, deliver(): return lax.ppermute(pair, ('tm', 'tk'), perm)  1.69 us
  transfers between devices with their start and end apart: 14, of which 8 were waited for; matrix products, arithmetic and copies ran while one was open for 1% of the time, Pallas kernels for 37%

profile of v1, /device:TPU:0, one launch (start us, length us, event | category | flops | bytes accessed | tf_op | source)
XLA Modules:
  0.0 68.8 jit_solution(1029198914832472004)
XLA Ops:
  0.0 0.0 copy-start
  0.0 0.0 copy-start.1
  0.0 5.1 %collective-permute-start.2 = (bf16[32,2048]{1,0:T(8,128)(2,1)}, bf16[32,2048]{1,0:T(8,128)(2,1)S(1)}, u32[]{:S(2)}, u32[]{:S(2)}) collective-permute-start(bf16[32,2048]{1,0:T(8,128)(2,1)} %bitcast.5), channel_id=1, source_target_pairs={{0,12},{4,8},{8,4},{12,0},{1,13},{5,9},{9,5},{13,1},{2,14},{6,10},... | collective-permute-start | bytes 393224 | tf_op jit(solution)/shard_map/ppermute | solution.py:289
  5.1 0.0 collective-permute-start.1
  5.1 0.6 collective-permute-start
  5.8 10.2 %load.1 = (bf16[2048,128]{1,0:T(8,128)(2,1)S(1)}, bf16[64,7168]{1,0:T(8,128)(2,1)S(1)}, bf16[64,7168]{1,0:T(8,128)(2,1)S(1)}, bf16[2048,1024]{1,0:T(8,128)(2,1)S...) custom-call(bf16[1,2048,128]{2,1,0:T(8,128)(2,1)} %refs_0_.1, ...), custom_call_target="tpu_custom_call" | custom-call | bytes 63438848 | tf_op jit(solution)/shard_map/load/pallas_call | solution.py:190
  16.0 0.0 collective-permute-done.2.three
  16.0 0.4 collective-permute-done.1.two
  16.4 0.0 collective-permute-done.one
  16.4 0.0 copy-done
  16.4 0.3 assemble_and_shrink.1
  16.8 0.1 collective-permute-start.3
  16.8 1.2 %collective-permute-done.3 = f32[128,128]{1,0:T(8,128)S(1)} collective-permute-done((f32[128,128]{1,0:T(8,128)S(1)}, f32[128,128]{1,0:T(8,128)S(1)}, u32[]{:S(2)}, u32[]{:S(2)}) %collective-permute-start.3) | collective-permute-done | bytes 65568 | tf_op jit(solution)/shard_map/ppermute | solution.py:289
  18.1 1.0 %collective-permute-start.5 = (f32[128,128]{1,0:T(8,128)S(1)}, f32[128,128]{1,0:T(8,128)S(1)}, u32[]{:S(2)}, u32[]{:S(2)}) collective-permute-start(f32[128,128]{1,0:T(8,128)S(1)} %add.53), channel_id=1, source_target_pairs={{0,4},{1,12},{2,0},{3,8},{4,5},{5,13},{6,1},{7,9},{8,6},{9,14},{10... | collective-permute-start | bytes 196616 | tf_op jit(solution)/shard_map/ppermute | solution.py:312
  19.1 0.7 collective-permute-start.4
  19.8 2.6 %collective-permute-done.5.second = f32[128,128]{1,0:T(8,128)S(1)} collective-permute-done((f32[128,128]{1,0:T(8,128)S(1)}, f32[128,128]{1,0:T(8,128)S(1)}, u32[]{:S(2)}, u32[]{:S(2)}) %collective-permute-start.5) | collective-permute-done | bytes 65568 | tf_op jit(solution)/shard_map/ppermute | solution.py:312
  22.4 0.0 collective-permute-done.4.first
  22.4 0.0 copy-done.1
  22.4 0.0 copy-done.2
  22.4 0.6 spread.1.ranks_ref
  23.0 2.9 %product.4 = (bf16[128,1024]{1,0:T(8,128)(2,1)S(1)}, f32[128,1024]{1,0:T(8,128)S(1)}) custom-call(bf16[128,2048]{1,0:T(8,128)(2,1)S(1)} %get-tuple-element.41.x_ref, bf16[128,128]{1,0:T(8,128)(2,1)S(1)} %spread.1.ranks_ref, bf16[2048,1024]{1,0:T(8,128)(2,1)S(1)} %get-tuple-element.28.gate, bf16[2048,7168]{1,0:T(8,128)(2,1)} %up.7, ...), custom_call_target="tpu_custom_call" | custom-call | flops 1073741824 | bytes 8388608 | tf_op jit(solution)/shard_map/product/pallas_call | solution.py:246
  25.9 4.8 %collective-permute-start.6 = (bf16[128,1024]{1,0:T(8,128)(2,1)S(1)}, bf16[128,1024]{1,0:T(8,128)(2,1)S(1)}, u32[]{:S(2)}, u32[]{:S(2)}) collective-permute-start(bf16[128,1024]{1,0:T(8,128)(2,1)S(1)} %get-tuple-element.32), channel_id=1, source_target_pairs={{0,1},{1,0},{2,3},{3,2},{4,5},{5,4},{6,7},{7,6},{8,9},{9,8},{10,11... | collective-permute-start | bytes 786440 | tf_op jit(solution)/shard_map/ppermute | solution.py:289
  30.8 1.2 %collective-permute-done.6 = bf16[128,1024]{1,0:T(8,128)(2,1)S(1)} collective-permute-done((bf16[128,1024]{1,0:T(8,128)(2,1)S(1)}, bf16[128,1024]{1,0:T(8,128)(2,1)S(1)}, u32[]{:S(2)}, u32[]{:S(2)}) %collective-permute-start.6) | collective-permute-done | bytes 262176 | tf_op jit(solution)/shard_map/ppermute | solution.py:289
  32.0 2.8 %collective-permute-start.7 = (bf16[64,1024]{1,0:T(8,128)(2,1)S(1)}, bf16[64,1024]{1,0:T(8,128)(2,1)S(1)}, u32[]{:S(2)}, u32[]{:S(2)}) collective-permute-start(bf16[64,1024]{1,0:T(8,128)(2,1)S(1)} %add_convert_fusion.3), channel_id=1, source_target_pairs={{0,2},{1,3},{2,0},{3,1},{4,6},{5,7},{6,4},{7,5},{8,10},{9,11},{10,... | collective-permute-start | bytes 393224 | tf_op jit(solution)/shard_map/ppermute | solution.py:289
  34.7 5.1 %product.6 = (bf16[128,2048]{1,0:T(8,128)(2,1)S(1)}, f32[128,2048]{1,0:T(8,128)S(1)}) custom-call(bf16[128,2048]{1,0:T(8,128)(2,1)S(1)} %get-tuple-element.41.x_ref, bf16[128,128]{1,0:T(8,128)(2,1)S(1)} %spread.1.ranks_ref, bf16[2048,2048]{1,0:T(8,128)(2,1)S(1)} %get-tuple-element.38.gate, bf16[2048,7168]{1,0:T(8,128)(2,1)} %up.7, ...), custom_call_target="tpu_custom_call" | custom-call | flops 2147483648 | bytes 16777216 | tf_op jit(solution)/shard_map/product/pallas_call | solution.py:246
  39.8 0.2 collective-permute-start.10
  40.0 5.1 %product.5 = (bf16[128,2048]{1,0:T(8,128)(2,1)S(1)}, f32[128,2048]{1,0:T(8,128)S(1)}) custom-call(bf16[128,2048]{1,0:T(8,128)(2,1)S(1)} %get-tuple-element.41.x_ref, bf16[128,128]{1,0:T(8,128)(2,1)S(1)} %spread.1.ranks_ref, bf16[2048,2048]{1,0:T(8,128)(2,1)S(1)} %get-tuple-element.34.gate, bf16[2048,7168]{1,0:T(8,128)(2,1)} %up.7, ...), custom_call_target="tpu_custom_call" | custom-call | flops 2147483648 | bytes 16777216 | tf_op jit(solution)/shard_map/product/pallas_call | solution.py:246
  45.1 0.5 collective-permute-start.8
  45.6 0.0 collective-permute-done.7
  45.7 0.0 collective-permute-done.10
  45.7 0.1 collective-permute-start.11
  45.8 1.3 %collective-permute-done.8 = bf16[128,2048]{1,0:T(8,128)(2,1)S(1)} collective-permute-done((bf16[128,2048]{1,0:T(8,128)(2,1)S(1)}, bf16[128,2048]{1,0:T(8,128)(2,1)S(1)}, u32[]{:S(2)}, u32[]{:S(2)}) %collective-permute-start.8) | collective-permute-done | bytes 524320 | tf_op jit(solution)/shard_map/ppermute | solution.py:289
  47.1 0.8 %collective-permute-start.9 = (bf16[64,2048]{1,0:T(8,128)(2,1)S(1)}, bf16[64,2048]{1,0:T(8,128)(2,1)S(1)}, u32[]{:S(2)}, u32[]{:S(2)}) collective-permute-start(bf16[64,2048]{1,0:T(8,128)(2,1)S(1)} %add_convert_fusion.2), channel_id=1, source_target_pairs={{0,2},{1,3},{2,0},{3,1},{4,6},{5,7},{6,4},{7,5},{8,10},{9,11},{10,... | collective-permute-start | bytes 786440 | tf_op jit(solution)/shard_map/ppermute | solution.py:289
  47.9 5.1 %product.7 = (bf16[128,2048]{1,0:T(8,128)(2,1)S(1)}, f32[128,2048]{1,0:T(8,128)S(1)}) custom-call(bf16[128,2048]{1,0:T(8,128)(2,1)S(1)} %get-tuple-element.41.x_ref, bf16[128,128]{1,0:T(8,128)(2,1)S(1)} %spread.1.ranks_ref, bf16[2048,2048]{1,0:T(8,128)(2,1)S(1)} %get-tuple-element.42.gate, bf16[2048,7168]{1,0:T(8,128)(2,1)} %up.7, ...), custom_call_target="tpu_custom_call" | custom-call | flops 2147483648 | bytes 16777216 | tf_op jit(solution)/shard_map/product/pallas_call | solution.py:246
  53.0 0.1 collective-permute-start.12
  53.1 1.8 %collective-permute-done.11 = bf16[64,2048]{1,0:T(8,128)(2,1)S(1)} collective-permute-done((bf16[64,2048]{1,0:T(8,128)(2,1)S(1)}, bf16[64,2048]{1,0:T(8,128)(2,1)S(1)}, u32[]{:S(2)}, u32[]{:S(2)}) %collective-permute-start.11) | collective-permute-done | bytes 262176 | tf_op jit(solution)/shard_map/ppermute | solution.py:289
  55.0 0.1 convert_add_fusion.1
  55.0 0.1 fusion.1
  55.1 4.6 %collective-permute-done.9 = bf16[64,2048]{1,0:T(8,128)(2,1)S(1)} collective-permute-done((bf16[64,2048]{1,0:T(8,128)(2,1)S(1)}, bf16[64,2048]{1,0:T(8,128)(2,1)S(1)}, u32[]{:S(2)}, u32[]{:S(2)}) %collective-permute-start.9) | collective-permute-done | bytes 262176 | tf_op jit(solution)/shard_map/ppermute | solution.py:289
  59.7 0.1 convert_add_fusion.2
  59.8 0.0 collective-permute-done.12
  59.8 0.1 add_convert_fusion
  59.9 0.4 collective-permute-start.13
  60.2 0.1 fusion.2
  60.3 7.1 %collective-permute-done.13 = bf16[64,2048]{1,0:T(8,128)(2,1)S(1)} collective-permute-done((bf16[64,2048]{1,0:T(8,128)(2,1)S(1)}, bf16[64,2048]{1,0:T(8,128)(2,1)S(1)}, u32[]{:S(2)}, u32[]{:S(2)}) %collective-permute-start.13) | collective-permute-done | bytes 262176 | tf_op jit(solution)/shard_map/ppermute | solution.py:289
  67.4 0.1 convert_add_fusion
  67.5 0.1 fusion
  67.6 1.2 %copy.11 = bf16[2,16,7168]{2,0,1:T(2,128)(2,1)} copy(bf16[2,16,7168]{2,1,0:T(8,128)(2,1)S(1)} %bitcast.9) | data formatting | bytes 917504 | tf_op jit(solution)/shard_map/reshape | solution.py:332
  (8 shorter events, 0.3 us)
Async XLA Ops:
  0.0 16.4 %copy-start = (bf16[2,16,2048]{2,1,0:T(8,128)(2,1)S(1)}, bf16[2,16,2048]{2,1,0:T(8,128)(2,1)}, u32[]{:S(2)}) copy-start(bf16[2,16,2048]{2,1,0:T(8,128)(2,1)} %param.8) | copy-start | bytes 393220
  0.0 22.4 %copy-start.1 = (s32[2,8]{1,0:T(2,128)S(1)}, s32[2,8]{1,0:T(2,128)}, u32[]{:S(2)}) copy-start(s32[2,8]{1,0:T(2,128)} %adapter_ref.1) | copy-start | bytes 196
  0.0 22.4 %copy-start.2 = (s32[4]{0:T(128)S(1)}, s32[4]{0:T(128)}, u32[]{:S(2)}) copy-start(s32[4]{0:T(128)} %slot_ref.1) | copy-start | bytes 52
  0.0 16.0 %collective-permute-start.2 = (bf16[32,2048]{1,0:T(8,128)(2,1)}, bf16[32,2048]{1,0:T(8,128)(2,1)S(1)}, u32[]{:S(2)}, u32[]{:S(2)}) collective-permute-start(bf16[32,2048]{1,0:T(8,128)(2,1)} %bitcast.5), channel_id=1, source_target_pairs={{0,12},{4,8},{8,4},{12,0},{1,13},{5,9},{9,5},{13,1},{2,14},{6,10},... | collective-permute-start | bytes 393224 | tf_op jit(solution)/shard_map/ppermute | solution.py:289
  5.1 11.3 %collective-permute-start.1 = (bf16[32,2048]{1,0:T(8,128)(2,1)}, bf16[32,2048]{1,0:T(8,128)(2,1)S(1)}, u32[]{:S(2)}, u32[]{:S(2)}) collective-permute-start(bf16[32,2048]{1,0:T(8,128)(2,1)} %bitcast.6), channel_id=1, source_target_pairs={{0,8},{4,12},{8,0},{12,4},{1,9},{5,13},{9,1},{13,5},{2,10},{6,14},... | collective-permute-start | bytes 393224 | tf_op jit(solution)/shard_map/ppermute | solution.py:289
  5.1 11.3 %collective-permute-start = (bf16[32,2048]{1,0:T(8,128)(2,1)}, bf16[32,2048]{1,0:T(8,128)(2,1)S(1)}, u32[]{:S(2)}, u32[]{:S(2)}) collective-permute-start(bf16[32,2048]{1,0:T(8,128)(2,1)} %bitcast.7), channel_id=1, source_target_pairs={{0,4},{4,0},{8,12},{12,8},{1,5},{5,1},{9,13},{13,9},{2,6},{6,2},{1... | collective-permute-start | bytes 393224 | tf_op jit(solution)/shard_map/ppermute | solution.py:289
  16.8 1.3 %collective-permute-start.3 = (f32[128,128]{1,0:T(8,128)S(1)}, f32[128,128]{1,0:T(8,128)S(1)}, u32[]{:S(2)}, u32[]{:S(2)}) collective-permute-start(f32[128,128]{1,0:T(8,128)S(1)} %get-tuple-element.27), channel_id=1, source_target_pairs={{0,1},{1,0},{2,3},{3,2},{4,5},{5,4},{6,7},{7,6},{8,9},{9,8},{10,11... | collective-permute-start | bytes 196616 | tf_op jit(solution)/shard_map/ppermute | solution.py:289
  18.1 4.3 %collective-permute-start.5 = (f32[128,128]{1,0:T(8,128)S(1)}, f32[128,128]{1,0:T(8,128)S(1)}, u32[]{:S(2)}, u32[]{:S(2)}) collective-permute-start(f32[128,128]{1,0:T(8,128)S(1)} %add.53), channel_id=1, source_target_pairs={{0,4},{1,12},{2,0},{3,8},{4,5},{5,13},{6,1},{7,9},{8,6},{9,14},{10... | collective-permute-start | bytes 196616 | tf_op jit(solution)/shard_map/ppermute | solution.py:312
  19.1 3.3 %collective-permute-start.4 = (f32[128,128]{1,0:T(8,128)S(1)}, f32[128,128]{1,0:T(8,128)S(1)}, u32[]{:S(2)}, u32[]{:S(2)}) collective-permute-start(f32[128,128]{1,0:T(8,128)S(1)} %add.53), channel_id=1, source_target_pairs={{0,0},{1,8},{2,4},{3,12},{4,1},{5,9},{6,5},{7,13},{8,2},{9,10},{10... | collective-permute-start | bytes 196616 | tf_op jit(solution)/shard_map/ppermute | solution.py:312
  25.9 6.0 %collective-permute-start.6 = (bf16[128,1024]{1,0:T(8,128)(2,1)S(1)}, bf16[128,1024]{1,0:T(8,128)(2,1)S(1)}, u32[]{:S(2)}, u32[]{:S(2)}) collective-permute-start(bf16[128,1024]{1,0:T(8,128)(2,1)S(1)} %get-tuple-element.32), channel_id=1, source_target_pairs={{0,1},{1,0},{2,3},{3,2},{4,5},{5,4},{6,7},{7,6},{8,9},{9,8},{10,11... | collective-permute-start | bytes 786440 | tf_op jit(solution)/shard_map/ppermute | solution.py:289
  32.0 13.6 %collective-permute-start.7 = (bf16[64,1024]{1,0:T(8,128)(2,1)S(1)}, bf16[64,1024]{1,0:T(8,128)(2,1)S(1)}, u32[]{:S(2)}, u32[]{:S(2)}) collective-permute-start(bf16[64,1024]{1,0:T(8,128)(2,1)S(1)} %add_convert_fusion.3), channel_id=1, source_target_pairs={{0,2},{1,3},{2,0},{3,1},{4,6},{5,7},{6,4},{7,5},{8,10},{9,11},{10,... | collective-permute-start | bytes 393224 | tf_op jit(solution)/shard_map/ppermute | solution.py:289
  39.8 5.8 %collective-permute-start.10 = (bf16[128,2048]{1,0:T(8,128)(2,1)S(1)}, bf16[128,2048]{1,0:T(8,128)(2,1)S(1)}, u32[]{:S(2)}, u32[]{:S(2)}) collective-permute-start(bf16[128,2048]{1,0:T(8,128)(2,1)S(1)} %get-tuple-element.40), channel_id=1, source_target_pairs={{0,1},{1,0},{2,3},{3,2},{4,5},{5,4},{6,7},{7,6},{8,9},{9,8},{10,11... | collective-permute-start | bytes 1572872 | tf_op jit(solution)/shard_map/ppermute | solution.py:289
  45.1 2.0 %collective-permute-start.8 = (bf16[128,2048]{1,0:T(8,128)(2,1)S(1)}, bf16[128,2048]{1,0:T(8,128)(2,1)S(1)}, u32[]{:S(2)}, u32[]{:S(2)}) collective-permute-start(bf16[128,2048]{1,0:T(8,128)(2,1)S(1)} %get-tuple-element.36), channel_id=1, source_target_pairs={{0,1},{1,0},{2,3},{3,2},{4,5},{5,4},{6,7},{7,6},{8,9},{9,8},{10,11... | collective-permute-start | bytes 1572872 | tf_op jit(solution)/shard_map/ppermute | solution.py:289
  45.7 9.2 %collective-permute-start.11 = (bf16[64,2048]{1,0:T(8,128)(2,1)S(1)}, bf16[64,2048]{1,0:T(8,128)(2,1)S(1)}, u32[]{:S(2)}, u32[]{:S(2)}) collective-permute-start(bf16[64,2048]{1,0:T(8,128)(2,1)S(1)} %add_convert_fusion.1), channel_id=1, source_target_pairs={{0,2},{1,3},{2,0},{3,1},{4,6},{5,7},{6,4},{7,5},{8,10},{9,11},{10,... | collective-permute-start | bytes 786440 | tf_op jit(solution)/shard_map/ppermute | solution.py:289
  47.1 12.6 %collective-permute-start.9 = (bf16[64,2048]{1,0:T(8,128)(2,1)S(1)}, bf16[64,2048]{1,0:T(8,128)(2,1)S(1)}, u32[]{:S(2)}, u32[]{:S(2)}) collective-permute-start(bf16[64,2048]{1,0:T(8,128)(2,1)S(1)} %add_convert_fusion.2), channel_id=1, source_target_pairs={{0,2},{1,3},{2,0},{3,1},{4,6},{5,7},{6,4},{7,5},{8,10},{9,11},{10,... | collective-permute-start | bytes 786440 | tf_op jit(solution)/shard_map/ppermute | solution.py:289
  53.0 6.7 %collective-permute-start.12 = (bf16[128,2048]{1,0:T(8,128)(2,1)S(1)}, bf16[128,2048]{1,0:T(8,128)(2,1)S(1)}, u32[]{:S(2)}, u32[]{:S(2)}) collective-permute-start(bf16[128,2048]{1,0:T(8,128)(2,1)S(1)} %get-tuple-element.44), channel_id=1, source_target_pairs={{0,1},{1,0},{2,3},{3,2},{4,5},{5,4},{6,7},{7,6},{8,9},{9,8},{10,11... | collective-permute-start | bytes 1572872 | tf_op jit(solution)/shard_map/ppermute | solution.py:289
  59.9 7.5 %collective-permute-start.13 = (bf16[64,2048]{1,0:T(8,128)(2,1)S(1)}, bf16[64,2048]{1,0:T(8,128)(2,1)S(1)}, u32[]{:S(2)}, u32[]{:S(2)}) collective-permute-start(bf16[64,2048]{1,0:T(8,128)(2,1)S(1)} %add_convert_fusion), channel_id=1, source_target_pairs={{0,2},{1,3},{2,0},{3,1},{4,6},{5,7},{6,4},{7,5},{8,10},{9,11},{10,... | collective-permute-start | bytes 786440 | tf_op jit(solution)/shard_map/ppermute | solution.py:289

commit v2 on v1

--- a/solution.py
+++ b/solution.py
@@ -11,7 +11,11 @@
 MIB = 2**20
 F32 = jnp.float32
 BF16 = jnp.bfloat16
-CHUNKS = (1024, 2048, 2048, 2048)
+CHUNKS = (2048, 1536, 2048, 1536)
+SLOTS = 5
+FAT = 10**11
+SPREAD = 10
+PTIES = (("pair",), ("mine",), ())
 TILE = 256
 
 
@@ -98,7 +102,8 @@
     ]
 
 
-def assemble_kernel(own, one, two, three, shrink, rows_out, part_out):
+def assemble_kernel(own, one, two, three, shrink, *refs):
+    rows_out, part_out = refs[-2:]
     z = lax.axis_index("tm")
     t = lax.axis_index("tk")
     size = own.shape[0]
@@ -113,13 +118,13 @@
         ]
 
 
-def assemble(pieces, shrink):
+def assemble(pieces, shrink, ties):
     rows = 4 * pieces[0].shape[0]
     depth, ranks = shrink.shape
     vmem = pl.BlockSpec(memory_space=pltpu.VMEM)
     return pl.pallas_call(
         assemble_kernel,
-        in_specs=[vmem] * 5,
+        in_specs=[vmem] * 5 + [pl.BlockSpec(memory_space=pl.ANY)] * len(ties),
         out_specs=[vmem] * 2,
         out_shape=[
             jax.ShapeDtypeStruct((rows, depth), BF16),
@@ -130,27 +135,41 @@
             flops=2 * rows * depth * ranks, bytes_accessed=2 * MIB, transcendentals=0
         ),
         name="assemble_and_shrink",
-    )(*pieces, shrink)
-
-
-def spread_kernel(blocks, adapter_ref, slot_ref, first, second, out):
+    )(*pieces, shrink, *ties)
+
+
+def spread_kernel(blocks, adapter_ref, slot_ref, mine, theirs, out):
     t = lax.axis_index("tk")
     steps = adapter_ref.shape[0]
-    size = first.shape[0] // 4
+    size = mine.shape[0] // 4
+    rank = mine.shape[1] // 2
     parts = []
-    for place in range(4):
+    for place in (1, 0):
         group = t ^ swap_bits(place)
         rows = pl.ds(pl.multiple_of(group * size, size), size)
-        total = first[rows, :] + second[rows, :]
+        pair = [ref[rows, :].astype(F32) for ref in (mine, theirs)]
         slots = block_slots(adapter_ref, slot_ref, group, steps, blocks)
         for i, slot in enumerate(slots):
-            here = total[i * BLOCK : (i + 1) * BLOCK]
-            parts.append(jnp.where(slot == t, here, jnp.zeros_like(here)))
+            here = []
+            for held, value in ((t, pair[0]), (t ^ 1, pair[1])):
+                block = value[i * BLOCK : (i + 1) * BLOCK]
+                here.append(jnp.where(slot == held, block, jnp.zeros_like(block)))
+            parts.append(
+                jnp.concatenate(
+                    [
+                        here[0][:, :rank],
+                        here[1][:, :rank],
+                        here[0][:, rank:],
+                        here[1][:, rank:],
+                    ],
+                    axis=1,
+                )
+            )
     out[...] = jnp.concatenate(parts, axis=0).astype(BF16)
 
 
-def spread(first, second, block_adapter, store_slot):
-    rows, ranks = first.shape
+def spread(mine, theirs, block_adapter, store_slot):
+    rows, ranks = mine.shape
     blocks = block_adapter.shape[1] // 4
     vmem = pl.BlockSpec(memory_space=pltpu.VMEM)
     smem = pl.BlockSpec(memory_space=pltpu.SMEM)
@@ -158,13 +177,147 @@
         functools.partial(spread_kernel, blocks),
         in_specs=[smem, smem, vmem, vmem],
         out_specs=vmem,
-        out_shape=jax.ShapeDtypeStruct((rows, ranks), BF16),
+        out_shape=jax.ShapeDtypeStruct((rows // 2, 2 * ranks), BF16),
+        compiler_params=pltpu.CompilerParams(vmem_limit_bytes=4 * MIB),
+        cost_estimate=pl.CostEstimate(flops=SPREAD, bytes_accessed=SPREAD // 1000, transcendentals=0),
+        name="spread",
+    )(block_adapter, store_slot, mine, theirs)
+
+
+def over_kernel(start, tile, ranks_ref, eg, eu, fg, fu, keep, got, *refs):
+    over, own = refs[-2:]
+    cols = keep.shape[1]
+    half = keep.shape[0] // 2
+    quarter = half // 2
+    wide = ranks_ref.shape[1] // 2
+    for j in range(cols // tile):
+        at = slice(j * tile, (j + 1) * tile)
+        there = slice(start + j * tile, start + (j + 1) * tile)
+        for which, (mine, theirs) in enumerate(((eg, fg), (eu, fu))):
+            expand = jnp.concatenate([mine[:, there], theirs[:, there]], axis=0)
+            y = jnp.dot(
+                ranks_ref[:, which * wide : (which + 1) * wide],
+                expand,
+                preferred_element_type=F32,
+            )
+            far_rows = slice(which * quarter, (which + 1) * quarter)
+            own_rows = slice(half + which * quarter, half + (which + 1) * quarter)
+            over[far_rows, at] = (
+                keep[far_rows, at] + got[far_rows, at].astype(F32) + y[:quarter]
+            ).astype(BF16)
+            own[far_rows, at] = (
+                keep[own_rows, at] + got[own_rows, at].astype(F32) + y[quarter:]
+            )
+
+
+def pair_sum(ranks, expands, keep, got, start, ties):
+    rows, cols = keep.shape
+    vmem = pl.BlockSpec(memory_space=pltpu.VMEM)
+    return pl.pallas_call(
+        functools.partial(over_kernel, start, TILE),
+        in_specs=[vmem] * 7 + [pl.BlockSpec(memory_space=pl.ANY)] * len(ties),
+        out_specs=[vmem] * 2,
+        out_shape=[
+            pltpu.VMEM((rows // 2, cols), BF16),
+            pltpu.VMEM((rows // 2, cols), F32),
+        ],
         compiler_params=pltpu.CompilerParams(vmem_limit_bytes=4 * MIB),
         cost_estimate=pl.CostEstimate(
-            flops=2 * rows * ranks, bytes_accessed=rows * ranks * 10, transcendentals=0
+            flops=1,
+            bytes_accessed=1,
+            transcendentals=0,
         ),
-        name="spread",
-    )(block_adapter, store_slot, first, second)
+        name="pair_sum",
+    )(ranks, *[near(e) for e in expands], keep, got, *ties)
+
+
+def finish_kernel(start, tile, own, other, before, *refs):
+    del before
+    out, block, sem = refs[-3:]
+    cols = own.shape[1]
+    quarter = own.shape[0] // 2
+    here = quarter // 2
+    for j in range(cols // tile):
+        at = slice(j * tile, (j + 1) * tile)
+        total = own[:, at] + other[:, at].astype(F32)
+        gate, up = total[:quarter], total[quarter:]
+        done = (gate / (1.0 + jnp.exp(-gate)) * up).astype(BF16)
+        for step in range(quarter // here):
+            block[:, step, at] = done[step * here : (step + 1) * here]
+    copy = pltpu.make_async_copy(block, out.at[:, :, pl.ds(start, cols)], sem)
+    copy.start()
+    copy.wait()
+
+
+def finish(own, other, before, start, ties):
+    half, cols = own.shape
+    shape = before.shape
+    vmem = pl.BlockSpec(memory_space=pltpu.VMEM)
+    hbm = pl.BlockSpec(memory_space=pltpu.HBM)
+    return pl.pallas_call(
+        functools.partial(finish_kernel, start, TILE),
+        in_specs=[vmem, vmem, hbm] + [pl.BlockSpec(memory_space=pl.ANY)] * len(ties),
+        out_specs=hbm,
+        out_shape=jax.ShapeDtypeStruct(shape, BF16),
+        input_output_aliases={2: 0},
+        scratch_shapes=[
+            pltpu.VMEM((shape[0], shape[1], cols), BF16),
+            pltpu.SemaphoreType.DMA(()),
+        ],
+        compiler_params=pltpu.CompilerParams(vmem_limit_bytes=4 * MIB),
+        cost_estimate=pl.CostEstimate(
+            flops=1, bytes_accessed=1, transcendentals=0
+        ),
+        name="finish",
+    )(own, other, before, *ties)
+
+
+def join_kernel(first, second, out):
+    out[...] = (first[...] + second[...]).astype(BF16)
+
+
+def join(first, second):
+    vmem = pl.BlockSpec(memory_space=pltpu.VMEM)
+    return pl.pallas_call(
+        join_kernel,
+        in_specs=[vmem] * 2,
+        out_specs=vmem,
+        out_shape=jax.ShapeDtypeStruct(first.shape, BF16),
+        compiler_params=pltpu.CompilerParams(vmem_limit_bytes=2 * MIB),
+        cost_estimate=pl.CostEstimate(flops=FAT, bytes_accessed=FAT // 1000, transcendentals=0),
+        name="join",
+    )(first, second)
+
+
+def after_kernel(*refs):
+    out = refs[-1]
+    out[...] = jnp.zeros_like(out)
+
+
+def after(*values):
+    return pl.pallas_call(
+        after_kernel,
+        in_specs=[pl.BlockSpec(memory_space=pl.ANY)] * len(values),
+        out_specs=pl.BlockSpec(memory_space=pltpu.VMEM),
+        out_shape=jax.ShapeDtypeStruct((8, 128), F32),
+        compiler_params=pltpu.CompilerParams(vmem_limit_bytes=2 * MIB),
+        cost_estimate=pl.CostEstimate(flops=FAT, bytes_accessed=FAT // 1000, transcendentals=0),
+        name="after",
+    )(*values)
+
+
+def blank_kernel(out):
+    del out
+
+
+def blank(shape):
+    return pl.pallas_call(
+        blank_kernel,
+        out_specs=pl.BlockSpec(memory_space=pltpu.HBM),
+        out_shape=jax.ShapeDtypeStruct(shape, BF16),
+        compiler_params=pltpu.CompilerParams(vmem_limit_bytes=2 * MIB),
+        name="blank",
+    )()
 
 
 def load_kernel(plan, *refs):
@@ -199,68 +352,65 @@
     )(*[far(a) for a in arrays])
 
 
-def product_kernel(
-    start, cols, fetch, tile, x_ref, ranks_ref, gate, up, eg, eu, send, keep, buffer, sem
-):
-    rank = ranks_ref.shape[1] // 2
-    rows = x_ref.shape[0]
+def product_kernel(start, fetch, tile, ties, x_ref, gate, up, *refs):
+    send, keep, buffer, sem = refs[ties:]
+    rows, cols = keep.shape
     half, quarter = rows // 2, rows // 4
+    slots = buffer.shape[0]
+    count = cols // fetch
 
     def copy(j):
         return pltpu.make_async_copy(
             up.at[:, pl.ds(start + j * fetch, fetch)],
-            buffer.at[:, pl.ds(j * fetch, fetch)],
-            sem.at[j],
+            buffer.at[j % slots],
+            sem.at[j % slots],
         )
 
-    for j in range(cols // fetch):
+    def multiply(which, weight, at):
+        base = which * quarter
+        y = jnp.dot(x_ref[...], weight, preferred_element_type=F32)
+        keep[base : base + quarter, at] = y[quarter:half]
+        keep[half + base : half + base + quarter, at] = y[:quarter]
+        send[base : base + quarter, at] = y[half + quarter :].astype(BF16)
+        send[half + base : half + base + quarter, at] = y[half : half + quarter].astype(BF16)
+
+    for j in range(min(slots, count)):
         copy(j).start()
-    for which in range(2):
-        base = which * quarter
-        for j in range(cols // tile):
-            at = slice(j * tile, (j + 1) * tile)
-            there = slice(start + j * tile, start + (j + 1) * tile)
-            if which == 0:
-                weight = gate[:, at]
-            else:
-                if j * tile % fetch == 0:
-                    copy(j * tile // fetch).wait()
-                weight = buffer[:, at]
-            y = jnp.dot(x_ref[...], weight, preferred_element_type=F32)
-            y += jnp.dot(
-                ranks_ref[:, which * rank : (which + 1) * rank],
-                (eg, eu)[which][:, there],
-                preferred_element_type=F32,
-            )
-            keep[base : base + quarter, at] = y[quarter:half]
-            keep[half + base : half + base + quarter, at] = y[:quarter]
-            send[base : base + quarter, at] = y[half + quarter :].astype(BF16)
-            send[half + base : half + base + quarter, at] = y[half : half + quarter].astype(BF16)
-
-
-def product(x, ranks, gate, up, eg, eu, start, cols):
+    for j in range(count):
+        places = [slice(j * fetch + k, j * fetch + k + tile) for k in range(0, fetch, tile)]
+        for at in places:
+            multiply(0, gate[:, at], at)
+        copy(j).wait()
+        for k, at in enumerate(places):
+            multiply(1, buffer[j % slots, :, k * tile : (k + 1) * tile], at)
+        if j + slots < count:
+            copy(j + slots).start()
+
+
+def product(x, gate, up, start, cols, ties):
     rows, depth = x.shape
-    fetch = 512 if cols % 512 == 0 else cols // 2
+    fetch = 512
+    slots = min(SLOTS, cols // fetch)
     vmem = pl.BlockSpec(memory_space=pltpu.VMEM)
     hbm = pl.BlockSpec(memory_space=pltpu.HBM)
     return pl.pallas_call(
-        functools.partial(product_kernel, start, cols, fetch, TILE),
-        in_specs=[vmem, vmem, vmem, hbm, vmem, vmem],
+        functools.partial(product_kernel, start, fetch, TILE, len(ties)),
+        in_specs=[vmem, vmem, hbm] + [pl.BlockSpec(memory_space=pl.ANY)] * len(ties),
         out_specs=[vmem, vmem],
         out_shape=[
             pltpu.VMEM((rows, cols), BF16),
             pltpu.VMEM((rows, cols), F32),
         ],
         scratch_shapes=[
-            pltpu.VMEM((depth, cols), BF16),
-            pltpu.SemaphoreType.DMA((cols // fetch,)),
+            pltpu.VMEM((slots, depth, fetch), BF16),
+            pltpu.SemaphoreType.DMA((slots,)),
         ],
-        compiler_params=pltpu.CompilerParams(vmem_limit_bytes=12 * MIB),
+        compiler_params=pltpu.CompilerParams(vmem_limit_bytes=14 * MIB),
         cost_estimate=pl.CostEstimate(
-            flops=4 * rows * depth * cols, bytes_accessed=4 * depth * cols, transcendentals=0
+            flops=1, bytes_accessed=1, transcendentals=0
         ),
         name="product",
-    )(x, ranks, near(gate), far(up), near(eg), near(eu))
+    )(x, near(gate), far(up), *ties)
 
 
 def near(value):
@@ -282,15 +432,17 @@
     store_slot,
 ):
     steps, here, depth = hidden_in.shape
-    own = hidden_in.reshape(steps * here, depth)
+    held = hidden_in.reshape(steps * here, depth)
     rows = 4 * steps * here
 
     def exchange(value, axis, bit):
         return lax.ppermute(value, axis, [(i, i ^ bit) for i in range(4)])
 
-    three = exchange(own, "tm", 3)
-    two = exchange(own, "tm", 2)
-    one = exchange(own, "tm", 1)
+    fg = exchange(expand_gate[0], "tk", 1)
+    fu = exchange(expand_up[0], "tk", 1)
+    three = exchange(held, "tm", 3)
+    two = exchange(held, "tm", 2)
+    one = exchange(held, "tm", 1)
     plan = [(0, None, None), (1, None, None), (2, None, None)]
     start = 0
     for cols in CHUNKS:
@@ -299,7 +451,7 @@
     shrink, eg, eu, *gates = load(
         tuple(plan), shrink_store, expand_gate, expand_up, gate_weight
     )
-    x, part = assemble((own, one, two, three), shrink)
+    x, part = assemble((held, one, two, three), shrink, (fg, fu))
 
     pair = part + exchange(part, "tk", 1)
 
@@ -311,26 +463,30 @@
                 perm.append((a * 4 + t, (2 * core + (chip ^ j)) * 4 + a))
         return lax.ppermute(pair, ("tm", "tk"), perm)
 
-    ranks = spread(deliver(0), deliver(1), block_adapter, store_slot)
-
-    half, quarter = rows // 2, rows // 4
-    outs = []
+    mine = join(deliver(0), deliver(1))
+
+    theirs = exchange(mine, "tk", 1)
+    ranks = spread(mine, theirs, block_adapter, store_slot)
+    out = blank((here, steps, sum(CHUNKS)))
+
+    overs, owns, others, sends = [], [], [], []
     start = 0
-    overs = []
     for j, cols in enumerate(CHUNKS):
-        if j > 0:
-            x, _ = lax.optimization_barrier((x, overs[max(j - 2, 0)]))
-        send, keep = product(x, ranks, gates[j], up_weight, eg, eu, start, cols)
+        ties = ((pair,), (mine, *sends[:1]), overs[:2], sends[2:3])[j]
+        send, keep = product(x, gates[j], up_weight, start, cols, ties)
+        sends.append(send)
         got = exchange(send, "tk", 1)
-        over = (keep[:half] + got[:half]).astype(BF16)
+        ties = ((), overs[:1], (after(*others),) if j == 2 else (), overs[2:3])[j]
+        over, own = pair_sum(ranks, (eg, eu, fg, fu), keep, got, start, ties)
         overs.append(over)
-        other = exchange(over, "tk", 2)
-        total = keep[half:] + got[half:] + other
-        gate, up = total[:quarter], total[quarter:]
-        outs.append((jax.nn.silu(gate) * up).astype(BF16))
+        owns.append(own)
+        others.append(exchange(over, "tk", 2))
         start += cols
-    out = jnp.concatenate(outs, axis=1).reshape(steps, here, -1)
-    return jnp.transpose(out, (1, 0, 2))
+    start = 0
+    for j, cols in enumerate(CHUNKS):
+        out = finish(owns[j], others[j], out, start, overs[-1:])
+        start += cols
+    return out
 
 
 def solution(mesh):

time: 69 us -> 61.4 us (0.89)
  waiting for transfers between devices: 20.2 us -> 11.2 us
  Pallas kernels: 29.3 us -> 31.4 us
  starting transfers between devices: 17 us -> 18.4 us
  local copies, waits for them, and re-layouts: 1.25 us -> 0.02 us
  other arithmetic: 0.81 us -> 0.01 us
    ppermute x12 -> x15, waiting for transfers between devices: 17.6 us -> 11.2 us  [exchange(): return lax.ppermute(value, axis, [(i, i ^ bit) for i in range(4)])]
    ppermute x2, waiting for transfers between devices: 2.64 us -> 0.01 us  [deliver(): return lax.ppermute(pair, ('tm', 'tk'), perm)]
    ppermute x2, starting transfers between devices: 1.69 us -> 4.12 us  [deliver(): return lax.ppermute(pair, ('tm', 'tk'), perm)]
    pallas_call x5 -> x16, Pallas kernels: 18.5 us -> 20.5 us  [the longest x4 15.6 us: product(): pl.pallas_call(functools.partial(product_kernel, start, fetch, TILE, len(...]
    reshape x1 -> x0, local copies, waits for them, and re-layouts: 1.24 us -> none  [on_pairs(): out = jnp.concatenate(outs, axis=1).reshape(steps, here, -1)]
    ppermute x12 -> x15, starting transfers between devices: 15.4 us -> 14.3 us  [exchange(): return lax.ppermute(value, axis, [(i, i ^ bit) for i in range(4)])]
  transfers between devices with their start and end apart: 14 -> 17, of which waited for: 8 -> 6; matrix products, arithmetic and copies ran while one was open for 1% -> 0% of each run, Pallas kernels for 37% -> 49%
where the time goes in v2:
time: 61.4 us; the launch traced here: 61.3 us
  Pallas kernels  31.4 us (51%)
  starting transfers between devices  18.4 us (30%)
  waiting for transfers between devices  11.2 us (18%)
    pallas_call x4, Pallas kernels, product(): pl.pallas_call(functools.partial(product_kernel, start, fetch, TILE, len(...  15.6 us
    ppermute x15, starting transfers between devices, exchange(): return lax.ppermute(value, axis, [(i, i ^ bit) for i in range(4)])  14.3 us
    ppermute x15, waiting for transfers between devices, exchange(): return lax.ppermute(value, axis, [(i, i ^ bit) for i in range(4)])  11.2 us
    pallas_call x1, Pallas kernels, load(): pl.pallas_call(functools.partial(load_kernel, plan), in_specs=[pl.BlockSp...  10.2 us
    ppermute x2, starting transfers between devices, deliver(): return lax.ppermute(pair, ('tm', 'tk'), perm)  4.12 us
    pallas_call x4, Pallas kernels, finish(): pl.pallas_call(functools.partial(finish_kernel, start, TILE), in_specs=[v...  3.5 us
  transfers between devices with their start and end apart: 17, of which 6 were waited for; matrix products, arithmetic and copies ran while one was open for 0% of the time, Pallas kernels for 49%

profile of v2, /device:TPU:0, one launch (start us, length us, event | category | flops | bytes accessed | tf_op | source)
XLA Modules:
  0.0 61.3 jit_solution(3525785252339403181)
XLA Ops:
  0.0 0.5 collective-permute-start.3
  0.5 0.1 collective-permute-start.4
  0.5 3.0 %collective-permute-start = (bf16[32,2048]{1,0:T(8,128)(2,1)}, bf16[32,2048]{1,0:T(8,128)(2,1)S(1)}, u32[]{:S(2)}, u32[]{:S(2)}) collective-permute-start(bf16[32,2048]{1,0:T(8,128)(2,1)} %bitcast.3), channel_id=1, source_target_pairs={{0,4},{4,0},{8,12},{12,8},{1,5},{5,1},{9,13},{13,9},{2,6},{6,2},{1... | collective-permute-start | bytes 393224 | tf_op jit(solution)/shard_map/ppermute | solution.py:439
  3.5 2.6 %collective-permute-start.1 = (bf16[32,2048]{1,0:T(8,128)(2,1)}, bf16[32,2048]{1,0:T(8,128)(2,1)S(1)}, u32[]{:S(2)}, u32[]{:S(2)}) collective-permute-start(bf16[32,2048]{1,0:T(8,128)(2,1)} %bitcast.4), channel_id=1, source_target_pairs={{0,8},{4,12},{8,0},{12,4},{1,9},{5,13},{9,1},{13,5},{2,10},{6,14},... | collective-permute-start | bytes 393224 | tf_op jit(solution)/shard_map/ppermute | solution.py:439
  6.1 0.0 collective-permute-start.2
  6.1 10.2 %load.1 = (bf16[2048,128]{1,0:T(8,128)(2,1)S(1)}, bf16[64,7168]{1,0:T(8,128)(2,1)S(1)}, bf16[64,7168]{1,0:T(8,128)(2,1)S(1)}, bf16[2048,2048]{1,0:T(8,128)(2,1)S...) custom-call(bf16[1,2048,128]{2,1,0:T(8,128)(2,1)} %refs_0_.1, ...), custom_call_target="tpu_custom_call" | custom-call | bytes 63438848 | tf_op jit(solution)/shard_map/load/pallas_call | solution.py:343
  16.3 0.0 collective-permute-done.one
  16.3 0.3 collective-permute-done.1.two
  16.7 0.0 collective-permute-done.2.three
  16.7 0.0 collective-permute-done.3.refs_0_.fg
  16.7 0.0 collective-permute-done.4.refs_1_.fu
  16.7 0.3 assemble_and_shrink.1
  17.0 0.1 collective-permute-start.5
  17.1 1.2 %collective-permute-done.5 = f32[128,128]{1,0:T(8,128)S(1)} collective-permute-done((f32[128,128]{1,0:T(8,128)S(1)}, f32[128,128]{1,0:T(8,128)S(1)}, u32[]{:S(2)}, u32[]{:S(2)}) %collective-permute-start.5) | collective-permute-done | bytes 65568 | tf_op jit(solution)/shard_map/ppermute | solution.py:439
  18.3 0.7 %collective-permute-start.6 = (f32[128,128]{1,0:T(8,128)S(1)}, f32[128,128]{1,0:T(8,128)S(1)}, u32[]{:S(2)}, u32[]{:S(2)}) collective-permute-start(f32[128,128]{1,0:T(8,128)S(1)} %add.3.refs_0_), channel_id=1, source_target_pairs={{0,0},{1,8},{2,4},{3,12},{4,1},{5,9},{6,5},{7,13},{8,2},{9,10},{10... | collective-permute-start | bytes 196616 | tf_op jit(solution)/shard_map/ppermute | solution.py:464
  19.0 3.5 %collective-permute-start.7 = (f32[128,128]{1,0:T(8,128)S(1)}, f32[128,128]{1,0:T(8,128)S(1)}, u32[]{:S(2)}, u32[]{:S(2)}) collective-permute-start(f32[128,128]{1,0:T(8,128)S(1)} %add.3.refs_0_), channel_id=1, source_target_pairs={{0,4},{1,12},{2,0},{3,8},{4,5},{5,13},{6,1},{7,9},{8,6},{9,14},{10... | collective-permute-start | bytes 196616 | tf_op jit(solution)/shard_map/ppermute | solution.py:464
  22.5 4.3 %product.4 = (bf16[128,2048]{1,0:T(8,128)(2,1)S(1)}, f32[128,2048]{1,0:T(8,128)S(1)}) custom-call(bf16[128,2048]{1,0:T(8,128)(2,1)S(1)} %get-tuple-element.34.x_ref, bf16[2048,2048]{1,0:T(8,128)(2,1)S(1)} %get-tuple-element.37.gate, bf16[2048,7168]{1,0:T(8,128)(2,1)} %up.7, f32[128,128]{1,0:T(8,128)S(1)} %add.3.refs_0_), custom_call_target="tpu_custom_call" | custom-call | flops 1 | bytes 1 | tf_op jit(solution)/shard_map/product/pallas_call | solution.py:396
  26.8 2.5 %collective-permute-start.9 = (bf16[128,2048]{1,0:T(8,128)(2,1)S(1)}, bf16[128,2048]{1,0:T(8,128)(2,1)S(1)}, u32[]{:S(2)}, u32[]{:S(2)}) collective-permute-start(bf16[128,2048]{1,0:T(8,128)(2,1)S(1)} %get-tuple-element.39.refs_1_), channel_id=1, source_target_pairs={{0,1},{1,0},{2,3},{3,2},{4,5},{5,4},{6,7},{7,6},{8,9},{9,8},{10,11... | collective-permute-start | bytes 1572872 | tf_op jit(solution)/shard_map/ppermute | solution.py:439
  29.3 0.0 collective-permute-done.6.first
  29.3 0.0 collective-permute-done.7.second
  29.3 0.0 copy-start.1
  29.3 0.0 copy-start.2
  29.3 3.5 %product.5 = (bf16[128,1536]{1,0:T(8,128)(2,1)S(1)}, f32[128,1536]{1,0:T(8,128)S(1)}) custom-call(bf16[128,2048]{1,0:T(8,128)(2,1)S(1)} %get-tuple-element.34.x_ref, bf16[2048,1536]{1,0:T(8,128)(2,1)S(1)} %get-tuple-element.41.gate, bf16[2048,7168]{1,0:T(8,128)(2,1)} %up.7, bf16[128,128]{1,0:T(8,128)(2,1)S(1)} %join.1.mine.refs_0_, ...), custom_call_target="tpu_custom_call" | custom-call | flops 1 | bytes 1 | tf_op jit(solution)/shard_map/product/pallas_call | solution.py:396
  32.9 0.1 collective-permute-start.10
  33.0 0.5 collective-permute-start.8
  33.5 1.3 %collective-permute-done.8.theirs = bf16[128,128]{1,0:T(8,128)(2,1)S(1)} collective-permute-done((bf16[128,128]{1,0:T(8,128)(2,1)S(1)}, bf16[128,128]{1,0:T(8,128)(2,1)S(1)}, u32[]{:S(2)}, u32[]{:S(2)}) %collective-permute-start.8) | collective-permute-done | bytes 32800 | tf_op jit(solution)/shard_map/ppermute | solution.py:439
  34.7 0.7 %spread.1.ranks_ref = bf16[64,256]{1,0:T(8,128)(2,1)S(1)} custom-call(s32[2,8]{1,0:T(2,128)S(1)} %copy-done.1, s32[4]{0:T(128)S(1)} %copy-done.2, bf16[128,128]{1,0:T(8,128)(2,1)S(1)} %join.1.mine.refs_0_, bf16[128,128]{1,0:T(8,128)(2,1)S(1)} %collective-permute-done.8.theirs), custom_call_target="tpu_custom_call" | custom-call | flops 10 | tf_op jit(solution)/shard_map/spread/pallas_call | solution.py:176
  35.4 0.0 collective-permute-done.9.got
  35.4 0.3 pair_sum.4
  35.7 1.3 %collective-permute-start.13 = (bf16[64,2048]{1,0:T(8,128)(2,1)S(1)}, bf16[64,2048]{1,0:T(8,128)(2,1)S(1)}, u32[]{:S(2)}, u32[]{:S(2)}) collective-permute-start(bf16[64,2048]{1,0:T(8,128)(2,1)S(1)} %get-tuple-element.40.refs_0_), channel_id=1, source_target_pairs={{0,2},{1,3},{2,0},{3,1},{4,6},{5,7},{6,4},{7,5},{8,10},{9,11},{10,... | collective-permute-start | bytes 786440 | tf_op jit(solution)/shard_map/ppermute | solution.py:439
  37.0 0.0 collective-permute-done.10.got
  37.0 0.3 pair_sum.5
  37.3 0.9 %collective-permute-start.14 = (bf16[64,1536]{1,0:T(8,128)(2,1)S(1)}, bf16[64,1536]{1,0:T(8,128)(2,1)S(1)}, u32[]{:S(2)}, u32[]{:S(2)}) collective-permute-start(bf16[64,1536]{1,0:T(8,128)(2,1)S(1)} %get-tuple-element.44.refs_1_), channel_id=1, source_target_pairs={{0,2},{1,3},{2,0},{3,1},{4,6},{5,7},{6,4},{7,5},{8,10},{9,11},{10,... | collective-permute-start | bytes 589832 | tf_op jit(solution)/shard_map/ppermute | solution.py:439
  38.1 4.3 %product.6 = (bf16[128,2048]{1,0:T(8,128)(2,1)S(1)}, f32[128,2048]{1,0:T(8,128)S(1)}) custom-call(bf16[128,2048]{1,0:T(8,128)(2,1)S(1)} %get-tuple-element.34.x_ref, bf16[2048,2048]{1,0:T(8,128)(2,1)S(1)} %get-tuple-element.36.gate, bf16[2048,7168]{1,0:T(8,128)(2,1)} %up.7, bf16[64,2048]{1,0:T(8,128)(2,1)S(1)} %get-tuple-element.40.refs_0_, ...), custom_call_target="tpu_custom_call" | custom-call | flops 1 | bytes 1 | tf_op jit(solution)/shard_map/product/pallas_call | solution.py:396
  42.4 0.1 collective-permute-start.12
  42.5 3.5 %product.7 = (bf16[128,1536]{1,0:T(8,128)(2,1)S(1)}, f32[128,1536]{1,0:T(8,128)S(1)}) custom-call(bf16[128,2048]{1,0:T(8,128)(2,1)S(1)} %get-tuple-element.34.x_ref, bf16[2048,1536]{1,0:T(8,128)(2,1)S(1)} %get-tuple-element.35.gate, bf16[2048,7168]{1,0:T(8,128)(2,1)} %up.7, bf16[128,2048]{1,0:T(8,128)(2,1)S(1)} %get-tuple-element.45.refs_0_), custom_call_target="tpu_custom_call" | custom-call | flops 1 | bytes 1 | tf_op jit(solution)/shard_map/product/pallas_call | solution.py:396
  46.0 0.6 collective-permute-start.11
  46.6 1.7 %collective-permute-done.14.refs_1_.other = bf16[64,1536]{1,0:T(8,128)(2,1)S(1)} collective-permute-done((bf16[64,1536]{1,0:T(8,128)(2,1)S(1)}, bf16[64,1536]{1,0:T(8,128)(2,1)S(1)}, u32[]{:S(2)}, u32[]{:S(2)}) %collective-permute-start.14) | collective-permute-done | bytes 196640 | tf_op jit(solution)/shard_map/ppermute | solution.py:439
  48.3 0.3 pair_sum.6
  48.6 1.6 %collective-permute-start.16 = (bf16[64,2048]{1,0:T(8,128)(2,1)S(1)}, bf16[64,2048]{1,0:T(8,128)(2,1)S(1)}, u32[]{:S(2)}, u32[]{:S(2)}) collective-permute-start(bf16[64,2048]{1,0:T(8,128)(2,1)S(1)} %get-tuple-element.49.refs_0_), channel_id=1, source_target_pairs={{0,2},{1,3},{2,0},{3,1},{4,6},{5,7},{6,4},{7,5},{8,10},{9,11},{10,... | collective-permute-start | bytes 786440 | tf_op jit(solution)/shard_map/ppermute | solution.py:439
  50.2 0.3 pair_sum.7
  50.5 0.6 collective-permute-start.15
  51.1 0.9 %finish.4.before = bf16[16,2,7168]{2,1,0:T(2,128)(2,1)} custom-call(f32[64,2048]{1,0:T(8,128)S(1)} %get-tuple-element.54.own, bf16[64,2048]{1,0:T(8,128)(2,1)S(1)} %collective-permute-done.13.refs_0_.other, bf16[16,2,7168]{2,1,0:T(2,128)(2,1)} %blank.1.before, bf16[64,1536]{1,0:T(8,128)(2,1)S(1)} %get-tuple-element.51.refs_0_), custom_call_target="tpu_custom_call", output_to_operand_aliasing={{}: (2, {})} | custom-call | flops 1 | bytes 1 | tf_op jit(solution)/shard_map/finish/pallas_call | solution.py:257
  52.0 0.8 %finish.5.before = bf16[16,2,7168]{2,1,0:T(2,128)(2,1)} custom-call(f32[64,1536]{1,0:T(8,128)S(1)} %get-tuple-element.53.own, bf16[64,1536]{1,0:T(8,128)(2,1)S(1)} %collective-permute-done.14.refs_1_.other, bf16[16,2,7168]{2,1,0:T(2,128)(2,1)} %finish.4.before, bf16[64,1536]{1,0:T(8,128)(2,1)S(1)} %get-tuple-element.51.refs_0_), custom_call_target="tpu_custom_call", output_to_operand_aliasing={{}: (2, {})} | custom-call | flops 1 | bytes 1 | tf_op jit(solution)/shard_map/finish/pallas_call | solution.py:257
  52.8 5.1 %collective-permute-done.16.other = bf16[64,2048]{1,0:T(8,128)(2,1)S(1)} collective-permute-done((bf16[64,2048]{1,0:T(8,128)(2,1)S(1)}, bf16[64,2048]{1,0:T(8,128)(2,1)S(1)}, u32[]{:S(2)}, u32[]{:S(2)}) %collective-permute-start.16) | collective-permute-done | bytes 262176 | tf_op jit(solution)/shard_map/ppermute | solution.py:439
  57.9 0.9 %finish.6.before = bf16[16,2,7168]{2,1,0:T(2,128)(2,1)} custom-call(f32[64,2048]{1,0:T(8,128)S(1)} %get-tuple-element.52.own, bf16[64,2048]{1,0:T(8,128)(2,1)S(1)} %collective-permute-done.16.other, bf16[16,2,7168]{2,1,0:T(2,128)(2,1)} %finish.5.before, bf16[64,1536]{1,0:T(8,128)(2,1)S(1)} %get-tuple-element.51.refs_0_), custom_call_target="tpu_custom_call", output_to_operand_aliasing={{}: (2, {})} | custom-call | flops 1 | bytes 1 | tf_op jit(solution)/shard_map/finish/pallas_call | solution.py:257
  58.9 1.6 %collective-permute-done.15.other = bf16[64,1536]{1,0:T(8,128)(2,1)S(1)} collective-permute-done((bf16[64,1536]{1,0:T(8,128)(2,1)S(1)}, bf16[64,1536]{1,0:T(8,128)(2,1)S(1)}, u32[]{:S(2)}, u32[]{:S(2)}) %collective-permute-start.15) | collective-permute-done | bytes 196640 | tf_op jit(solution)/shard_map/ppermute | solution.py:439
  60.4 0.8 %finish.7 = bf16[16,2,7168]{2,1,0:T(2,128)(2,1)} custom-call(f32[64,1536]{1,0:T(8,128)S(1)} %get-tuple-element.50.own, bf16[64,1536]{1,0:T(8,128)(2,1)S(1)} %collective-permute-done.15.other, bf16[16,2,7168]{2,1,0:T(2,128)(2,1)} %finish.6.before, bf16[64,1536]{1,0:T(8,128)(2,1)S(1)} %get-tuple-element.51.refs_0_), custom_call_target="tpu_custom_call", output_to_operand_aliasing={{}: (2, {})} | custom-call | flops 1 | bytes 1 | tf_op jit(solution)/shard_map/finish/pallas_call | solution.py:257
  (11 shorter events, 0.0 us)
Async XLA Ops:
  0.0 16.7 %collective-permute-start.3 = (bf16[64,7168]{1,0:T(8,128)(2,1)}, bf16[64,7168]{1,0:T(8,128)(2,1)S(1)}, u32[]{:S(2)}, u32[]{:S(2)}) collective-permute-start(bf16[64,7168]{1,0:T(8,128)(2,1)} %bitcast.7), channel_id=1, source_target_pairs={{0,1},{1,0},{2,3},{3,2},{4,5},{5,4},{6,7},{7,6},{8,9},{9,8},{10,11... | collective-permute-start | bytes 2752520 | tf_op jit(solution)/shard_map/ppermute | solution.py:439
  0.5 16.2 %collective-permute-start.4 = (bf16[64,7168]{1,0:T(8,128)(2,1)}, bf16[64,7168]{1,0:T(8,128)(2,1)S(1)}, u32[]{:S(2)}, u32[]{:S(2)}) collective-permute-start(bf16[64,7168]{1,0:T(8,128)(2,1)} %bitcast.8), channel_id=1, source_target_pairs={{0,1},{1,0},{2,3},{3,2},{4,5},{5,4},{6,7},{7,6},{8,9},{9,8},{10,11... | collective-permute-start | bytes 2752520 | tf_op jit(solution)/shard_map/ppermute | solution.py:439
  0.5 16.2 %copy-start = (bf16[2,16,2048]{2,1,0:T(8,128)(2,1)S(1)}, bf16[2,16,2048]{2,1,0:T(8,128)(2,1)}, u32[]{:S(2)}) copy-start(bf16[2,16,2048]{2,1,0:T(8,128)(2,1)} %param.8) | copy-start | bytes 393220
  0.5 15.8 %collective-permute-start = (bf16[32,2048]{1,0:T(8,128)(2,1)}, bf16[32,2048]{1,0:T(8,128)(2,1)S(1)}, u32[]{:S(2)}, u32[]{:S(2)}) collective-permute-start(bf16[32,2048]{1,0:T(8,128)(2,1)} %bitcast.3), channel_id=1, source_target_pairs={{0,4},{4,0},{8,12},{12,8},{1,5},{5,1},{9,13},{13,9},{2,6},{6,2},{1... | collective-permute-start | bytes 393224 | tf_op jit(solution)/shard_map/ppermute | solution.py:439
  3.5 13.1 %collective-permute-start.1 = (bf16[32,2048]{1,0:T(8,128)(2,1)}, bf16[32,2048]{1,0:T(8,128)(2,1)S(1)}, u32[]{:S(2)}, u32[]{:S(2)}) collective-permute-start(bf16[32,2048]{1,0:T(8,128)(2,1)} %bitcast.4), channel_id=1, source_target_pairs={{0,8},{4,12},{8,0},{12,4},{1,9},{5,13},{9,1},{13,5},{2,10},{6,14},... | collective-permute-start | bytes 393224 | tf_op jit(solution)/shard_map/ppermute | solution.py:439
  6.1 10.5 %collective-permute-start.2 = (bf16[32,2048]{1,0:T(8,128)(2,1)}, bf16[32,2048]{1,0:T(8,128)(2,1)S(1)}, u32[]{:S(2)}, u32[]{:S(2)}) collective-permute-start(bf16[32,2048]{1,0:T(8,128)(2,1)} %bitcast.5), channel_id=1, source_target_pairs={{0,12},{4,8},{8,4},{12,0},{1,13},{5,9},{9,5},{13,1},{2,14},{6,10},... | collective-permute-start | bytes 393224 | tf_op jit(solution)/shard_map/ppermute | solution.py:439
  17.0 1.3 %collective-permute-start.5 = (f32[128,128]{1,0:T(8,128)S(1)}, f32[128,128]{1,0:T(8,128)S(1)}, u32[]{:S(2)}, u32[]{:S(2)}) collective-permute-start(f32[128,128]{1,0:T(8,128)S(1)} %get-tuple-element.31), channel_id=1, source_target_pairs={{0,1},{1,0},{2,3},{3,2},{4,5},{5,4},{6,7},{7,6},{8,9},{9,8},{10,11... | collective-permute-start | bytes 196616 | tf_op jit(solution)/shard_map/ppermute | solution.py:439
  18.3 11.0 %collective-permute-start.6 = (f32[128,128]{1,0:T(8,128)S(1)}, f32[128,128]{1,0:T(8,128)S(1)}, u32[]{:S(2)}, u32[]{:S(2)}) collective-permute-start(f32[128,128]{1,0:T(8,128)S(1)} %add.3.refs_0_), channel_id=1, source_target_pairs={{0,0},{1,8},{2,4},{3,12},{4,1},{5,9},{6,5},{7,13},{8,2},{9,10},{10... | collective-permute-start | bytes 196616 | tf_op jit(solution)/shard_map/ppermute | solution.py:464
  19.0 10.3 %collective-permute-start.7 = (f32[128,128]{1,0:T(8,128)S(1)}, f32[128,128]{1,0:T(8,128)S(1)}, u32[]{:S(2)}, u32[]{:S(2)}) collective-permute-start(f32[128,128]{1,0:T(8,128)S(1)} %add.3.refs_0_), channel_id=1, source_target_pairs={{0,4},{1,12},{2,0},{3,8},{4,5},{5,13},{6,1},{7,9},{8,6},{9,14},{10... | collective-permute-start | bytes 196616 | tf_op jit(solution)/shard_map/ppermute | solution.py:464
  26.8 8.6 %collective-permute-start.9 = (bf16[128,2048]{1,0:T(8,128)(2,1)S(1)}, bf16[128,2048]{1,0:T(8,128)(2,1)S(1)}, u32[]{:S(2)}, u32[]{:S(2)}) collective-permute-start(bf16[128,2048]{1,0:T(8,128)(2,1)S(1)} %get-tuple-element.39.refs_1_), channel_id=1, source_target_pairs={{0,1},{1,0},{2,3},{3,2},{4,5},{5,4},{6,7},{7,6},{8,9},{9,8},{10,11... | collective-permute-start | bytes 1572872 | tf_op jit(solution)/shard_map/ppermute | solution.py:439
  29.3 5.4 %copy-start.1 = (s32[2,8]{1,0:T(2,128)S(1)}, s32[2,8]{1,0:T(2,128)}, u32[]{:S(2)}) copy-start(s32[2,8]{1,0:T(2,128)} %adapter_ref.1) | copy-start | bytes 196
  29.3 5.4 %copy-start.2 = (s32[4]{0:T(128)S(1)}, s32[4]{0:T(128)}, u32[]{:S(2)}) copy-start(s32[4]{0:T(128)} %slot_ref.1) | copy-start | bytes 52
  32.9 4.1 %collective-permute-start.10 = (bf16[128,1536]{1,0:T(8,128)(2,1)S(1)}, bf16[128,1536]{1,0:T(8,128)(2,1)S(1)}, u32[]{:S(2)}, u32[]{:S(2)}) collective-permute-start(bf16[128,1536]{1,0:T(8,128)(2,1)S(1)} %get-tuple-element.43), channel_id=1, source_target_pairs={{0,1},{1,0},{2,3},{3,2},{4,5},{5,4},{6,7},{7,6},{8,9},{9,8},{10,11... | collective-permute-start | bytes 1179656 | tf_op jit(solution)/shard_map/ppermute | solution.py:439
  33.0 1.7 %collective-permute-start.8 = (bf16[128,128]{1,0:T(8,128)(2,1)S(1)}, bf16[128,128]{1,0:T(8,128)(2,1)S(1)}, u32[]{:S(2)}, u32[]{:S(2)}) collective-permute-start(bf16[128,128]{1,0:T(8,128)(2,1)S(1)} %join.1.mine.refs_0_), channel_id=1, source_target_pairs={{0,1},{1,0},{2,3},{3,2},{4,5},{5,4},{6,7},{7,6},{8,9},{9,8},{10,11... | collective-permute-start | bytes 98312 | tf_op jit(solution)/shard_map/ppermute | solution.py:439
  35.7 12.6 %collective-permute-start.13 = (bf16[64,2048]{1,0:T(8,128)(2,1)S(1)}, bf16[64,2048]{1,0:T(8,128)(2,1)S(1)}, u32[]{:S(2)}, u32[]{:S(2)}) collective-permute-start(bf16[64,2048]{1,0:T(8,128)(2,1)S(1)} %get-tuple-element.40.refs_0_), channel_id=1, source_target_pairs={{0,2},{1,3},{2,0},{3,1},{4,6},{5,7},{6,4},{7,5},{8,10},{9,11},{10,... | collective-permute-start | bytes 786440 | tf_op jit(solution)/shard_map/ppermute | solution.py:439
  37.3 11.0 %collective-permute-start.14 = (bf16[64,1536]{1,0:T(8,128)(2,1)S(1)}, bf16[64,1536]{1,0:T(8,128)(2,1)S(1)}, u32[]{:S(2)}, u32[]{:S(2)}) collective-permute-start(bf16[64,1536]{1,0:T(8,128)(2,1)S(1)} %get-tuple-element.44.refs_1_), channel_id=1, source_target_pairs={{0,2},{1,3},{2,0},{3,1},{4,6},{5,7},{6,4},{7,5},{8,10},{9,11},{10,... | collective-permute-start | bytes 589832 | tf_op jit(solution)/shard_map/ppermute | solution.py:439
  42.4 5.9 %collective-permute-start.12 = (bf16[128,2048]{1,0:T(8,128)(2,1)S(1)}, bf16[128,2048]{1,0:T(8,128)(2,1)S(1)}, u32[]{:S(2)}, u32[]{:S(2)}) collective-permute-start(bf16[128,2048]{1,0:T(8,128)(2,1)S(1)} %get-tuple-element.45.refs_0_), channel_id=1, source_target_pairs={{0,1},{1,0},{2,3},{3,2},{4,5},{5,4},{6,7},{7,6},{8,9},{9,8},{10,11... | collective-permute-start | bytes 1572872 | tf_op jit(solution)/shard_map/ppermute | solution.py:439
  46.0 4.2 %collective-permute-start.11 = (bf16[128,1536]{1,0:T(8,128)(2,1)S(1)}, bf16[128,1536]{1,0:T(8,128)(2,1)S(1)}, u32[]{:S(2)}, u32[]{:S(2)}) collective-permute-start(bf16[128,1536]{1,0:T(8,128)(2,1)S(1)} %get-tuple-element.47), channel_id=1, source_target_pairs={{0,1},{1,0},{2,3},{3,2},{4,5},{5,4},{6,7},{7,6},{8,9},{9,8},{10,11... | collective-permute-start | bytes 1179656 | tf_op jit(solution)/shard_map/ppermute | solution.py:439
  48.6 9.3 %collective-permute-start.16 = (bf16[64,2048]{1,0:T(8,128)(2,1)S(1)}, bf16[64,2048]{1,0:T(8,128)(2,1)S(1)}, u32[]{:S(2)}, u32[]{:S(2)}) collective-permute-start(bf16[64,2048]{1,0:T(8,128)(2,1)S(1)} %get-tuple-element.49.refs_0_), channel_id=1, source_target_pairs={{0,2},{1,3},{2,0},{3,1},{4,6},{5,7},{6,4},{7,5},{8,10},{9,11},{10,... | collective-permute-start | bytes 786440 | tf_op jit(solution)/shard_map/ppermute | solution.py:439
  50.5 10.0 %collective-permute-start.15 = (bf16[64,1536]{1,0:T(8,128)(2,1)S(1)}, bf16[64,1536]{1,0:T(8,128)(2,1)S(1)}, u32[]{:S(2)}, u32[]{:S(2)}) collective-permute-start(bf16[64,1536]{1,0:T(8,128)(2,1)S(1)} %get-tuple-element.51.refs_0_), channel_id=1, source_target_pairs={{0,2},{1,3},{2,0},{3,1},{4,6},{5,7},{6,4},{7,5},{8,10},{9,11},{10,... | collective-permute-start | bytes 589832 | tf_op jit(solution)/shard_map/ppermute | solution.py:439

commit v3 on v2

--- a/solution.py
+++ b/solution.py
@@ -13,8 +13,9 @@
 BF16 = jnp.bfloat16
 CHUNKS = (2048, 1536, 2048, 1536)
 SLOTS = 5
+LEAD = 2
 FAT = 10**11
-SPREAD = 10
+SPREAD = 10**11
 PTIES = (("pair",), ("mine",), ())
 TILE = 256
 
@@ -138,50 +139,35 @@
     )(*pieces, shrink, *ties)
 
 
-def spread_kernel(blocks, adapter_ref, slot_ref, mine, theirs, out):
+def spread_kernel(mask, mine, theirs, out):
     t = lax.axis_index("tk")
-    steps = adapter_ref.shape[0]
     size = mine.shape[0] // 4
     rank = mine.shape[1] // 2
-    parts = []
-    for place in (1, 0):
+    for half, place in enumerate((1, 0)):
         group = t ^ swap_bits(place)
         rows = pl.ds(pl.multiple_of(group * size, size), size)
-        pair = [ref[rows, :].astype(F32) for ref in (mine, theirs)]
-        slots = block_slots(adapter_ref, slot_ref, group, steps, blocks)
-        for i, slot in enumerate(slots):
-            here = []
-            for held, value in ((t, pair[0]), (t ^ 1, pair[1])):
-                block = value[i * BLOCK : (i + 1) * BLOCK]
-                here.append(jnp.where(slot == held, block, jnp.zeros_like(block)))
-            parts.append(
-                jnp.concatenate(
-                    [
-                        here[0][:, :rank],
-                        here[1][:, :rank],
-                        here[0][:, rank:],
-                        here[1][:, rank:],
-                    ],
-                    axis=1,
-                )
-            )
-    out[...] = jnp.concatenate(parts, axis=0).astype(BF16)
-
-
-def spread(mine, theirs, block_adapter, store_slot):
+        here = []
+        for i, ref in enumerate((mine, theirs)):
+            value = ref[rows, :].astype(F32)
+            chosen = mask[i, half * size : (half + 1) * size, :] > 0.5
+            here.append(jnp.where(chosen, value, jnp.zeros_like(value)))
+        out[half * size : (half + 1) * size, :] = jnp.concatenate(
+            [here[0][:, :rank], here[1][:, :rank], here[0][:, rank:], here[1][:, rank:]], axis=1
+        ).astype(BF16)
+
+
+def spread(mask, mine, theirs):
     rows, ranks = mine.shape
-    blocks = block_adapter.shape[1] // 4
     vmem = pl.BlockSpec(memory_space=pltpu.VMEM)
-    smem = pl.BlockSpec(memory_space=pltpu.SMEM)
-    return pl.pallas_call(
-        functools.partial(spread_kernel, blocks),
-        in_specs=[smem, smem, vmem, vmem],
+    return pl.pallas_call(
+        spread_kernel,
+        in_specs=[vmem] * 3,
         out_specs=vmem,
         out_shape=jax.ShapeDtypeStruct((rows // 2, 2 * ranks), BF16),
-        compiler_params=pltpu.CompilerParams(vmem_limit_bytes=4 * MIB),
+        compiler_params=pltpu.CompilerParams(vmem_limit_bytes=2 * MIB),
         cost_estimate=pl.CostEstimate(flops=SPREAD, bytes_accessed=SPREAD // 1000, transcendentals=0),
         name="spread",
-    )(block_adapter, store_slot, mine, theirs)
+    )(mask, mine, theirs)
 
 
 def over_kernel(start, tile, ranks_ref, eg, eu, fg, fu, keep, got, *refs):
@@ -272,21 +258,22 @@
     )(own, other, before, *ties)
 
 
-def join_kernel(first, second, out):
-    out[...] = (first[...] + second[...]).astype(BF16)
-
-
-def join(first, second):
+def join_kernel(first, second, *refs):
+    out = refs[-1]
+    out[...] = (first[...] + second[...]).astype(out.dtype)
+
+
+def join(first, second, dtype, ties):
     vmem = pl.BlockSpec(memory_space=pltpu.VMEM)
     return pl.pallas_call(
         join_kernel,
-        in_specs=[vmem] * 2,
+        in_specs=[vmem] * 2 + [pl.BlockSpec(memory_space=pl.ANY)] * len(ties),
         out_specs=vmem,
-        out_shape=jax.ShapeDtypeStruct(first.shape, BF16),
+        out_shape=jax.ShapeDtypeStruct(first.shape, dtype),
         compiler_params=pltpu.CompilerParams(vmem_limit_bytes=2 * MIB),
         cost_estimate=pl.CostEstimate(flops=FAT, bytes_accessed=FAT // 1000, transcendentals=0),
         name="join",
-    )(first, second)
+    )(first, second, *ties)
 
 
 def after_kernel(*refs):
@@ -352,6 +339,33 @@
     )(*[far(a) for a in arrays])
 
 
+def mask_kernel(blocks, adapter_ref, slot_ref, mask):
+    t = lax.axis_index("tk")
+    row = 0
+    for place in (1, 0):
+        group = t ^ swap_bits(place)
+        slots = block_slots(adapter_ref, slot_ref, group, adapter_ref.shape[0], blocks)
+        for slot in slots:
+            for i, held in enumerate((t, t ^ 1)):
+                value = jnp.where(slot == held, 1.0, 0.0)
+                mask[i, row : row + BLOCK, :] = jnp.full((BLOCK, mask.shape[2]), value, F32)
+            row += BLOCK
+
+
+def masks(block_adapter, store_slot, ranks):
+    blocks = block_adapter.shape[1] // 4
+    rows = 2 * block_adapter.shape[0] * blocks * BLOCK
+    return pl.pallas_call(
+        functools.partial(mask_kernel, blocks),
+        in_specs=[pl.BlockSpec(memory_space=pltpu.SMEM)] * 2,
+        out_specs=pl.BlockSpec(memory_space=pltpu.VMEM),
+        out_shape=jax.ShapeDtypeStruct((2, rows, ranks), F32),
+        compiler_params=pltpu.CompilerParams(vmem_limit_bytes=2 * MIB),
+        cost_estimate=pl.CostEstimate(flops=1, bytes_accessed=1, transcendentals=0),
+        name="masks",
+    )(block_adapter, store_slot)
+
+
 def product_kernel(start, fetch, tile, ties, x_ref, gate, up, *refs):
     send, keep, buffer, sem = refs[ties:]
     rows, cols = keep.shape
@@ -366,25 +380,32 @@
             sem.at[j % slots],
         )
 
-    def multiply(which, weight, at):
+    def multiply(which, j):
         base = which * quarter
-        y = jnp.dot(x_ref[...], weight, preferred_element_type=F32)
-        keep[base : base + quarter, at] = y[quarter:half]
-        keep[half + base : half + base + quarter, at] = y[:quarter]
-        send[base : base + quarter, at] = y[half + quarter :].astype(BF16)
-        send[half + base : half + base + quarter, at] = y[half : half + quarter].astype(BF16)
+        for k in range(0, fetch, tile):
+            at = slice(j * fetch + k, j * fetch + k + tile)
+            if which == 0:
+                weight = gate[:, at]
+            else:
+                weight = buffer[j % slots, :, k : k + tile]
+            y = jnp.dot(x_ref[...], weight, preferred_element_type=F32)
+            keep[base : base + quarter, at] = y[quarter:half]
+            keep[half + base : half + base + quarter, at] = y[:quarter]
+            send[base : base + quarter, at] = y[half + quarter :].astype(BF16)
+            send[half + base : half + base + quarter, at] = y[half : half + quarter].astype(BF16)
 
     for j in range(min(slots, count)):
         copy(j).start()
+    lead = min(LEAD, count)
+    for j in range(lead):
+        multiply(0, j)
     for j in range(count):
-        places = [slice(j * fetch + k, j * fetch + k + tile) for k in range(0, fetch, tile)]
-        for at in places:
-            multiply(0, gate[:, at], at)
         copy(j).wait()
-        for k, at in enumerate(places):
-            multiply(1, buffer[j % slots, :, k * tile : (k + 1) * tile], at)
+        multiply(1, j)
         if j + slots < count:
             copy(j + slots).start()
+        if j + lead < count:
+            multiply(0, j + lead)
 
 
 def product(x, gate, up, start, cols, ties):
@@ -406,9 +427,7 @@
             pltpu.SemaphoreType.DMA((slots,)),
         ],
         compiler_params=pltpu.CompilerParams(vmem_limit_bytes=14 * MIB),
-        cost_estimate=pl.CostEstimate(
-            flops=1, bytes_accessed=1, transcendentals=0
-        ),
+        cost_estimate=pl.CostEstimate(flops=1, bytes_accessed=1, transcendentals=0),
         name="product",
     )(x, near(gate), far(up), *ties)
 
@@ -444,16 +463,15 @@
     two = exchange(held, "tm", 2)
     one = exchange(held, "tm", 1)
     plan = [(0, None, None), (1, None, None), (2, None, None)]
-    start = 0
-    for cols in CHUNKS:
+    starts = [sum(CHUNKS[:j]) for j in range(len(CHUNKS))]
+    for start, cols in zip(starts, CHUNKS):
         plan.append((3, start, cols))
-        start += cols
     shrink, eg, eu, *gates = load(
         tuple(plan), shrink_store, expand_gate, expand_up, gate_weight
     )
     x, part = assemble((held, one, two, three), shrink, (fg, fu))
-
-    pair = part + exchange(part, "tk", 1)
+    mask = masks(block_adapter, store_slot, shrink_store.shape[2])
+    pair = join(part, exchange(part, "tk", 1), F32, (mask,))
 
     def deliver(j):
         perm = []
@@ -463,29 +481,39 @@
                 perm.append((a * 4 + t, (2 * core + (chip ^ j)) * 4 + a))
         return lax.ppermute(pair, ("tm", "tk"), perm)
 
-    mine = join(deliver(0), deliver(1))
-
-    theirs = exchange(mine, "tk", 1)
-    ranks = spread(mine, theirs, block_adapter, store_slot)
-    out = blank((here, steps, sum(CHUNKS)))
-
-    overs, owns, others, sends = [], [], [], []
-    start = 0
-    for j, cols in enumerate(CHUNKS):
-        ties = ((pair,), (mine, *sends[:1]), overs[:2], sends[2:3])[j]
-        send, keep = product(x, gates[j], up_weight, start, cols, ties)
+    sends, keeps, gots = [], [], []
+    overs, owns, others = [], [], []
+
+    def multiply(j, ties):
+        send, keep = product(
+            x, gates[j], up_weight, starts[j], CHUNKS[j], ties
+        )
         sends.append(send)
-        got = exchange(send, "tk", 1)
-        ties = ((), overs[:1], (after(*others),) if j == 2 else (), overs[2:3])[j]
-        over, own = pair_sum(ranks, (eg, eu, fg, fu), keep, got, start, ties)
+        keeps.append(keep)
+        gots.append(exchange(send, "tk", 1))
+
+    def add_pair(j, ties):
+        over, own = pair_sum(
+            ranks, (eg, eu, fg, fu), keeps[j], gots[j], starts[j], ties
+        )
         overs.append(over)
         owns.append(own)
         others.append(exchange(over, "tk", 2))
-        start += cols
-    start = 0
-    for j, cols in enumerate(CHUNKS):
-        out = finish(owns[j], others[j], out, start, overs[-1:])
-        start += cols
+
+    multiply(0, (pair,))
+    mine = join(deliver(0), deliver(1), BF16, (sends[0],))
+    theirs = exchange(mine, "tk", 1)
+    multiply(1, (mine,))
+    ranks = spread(mask, mine, theirs)
+    add_pair(0, (sends[1],))
+    add_pair(1, (overs[0],))
+    multiply(2, (overs[0], overs[1]))
+    multiply(3, (sends[2],))
+    add_pair(2, (after(others[0], others[1]),))
+    add_pair(3, (overs[2],))
+    out = blank((here, steps, sum(CHUNKS)))
+    for j in range(len(CHUNKS)):
+        out = finish(owns[j], others[j], out, starts[j], overs[-1:])
     return out
 
 

time: 61.4 us -> 59.4 us (0.967)
  waiting for transfers between devices: 11.2 us -> 9.21 us
  starting transfers between devices: 18.4 us -> 19.2 us
  Pallas kernels: 31.4 us -> 30.6 us
    ppermute x15, waiting for transfers between devices: 11.2 us -> 9.21 us  [exchange(): return lax.ppermute(value, axis, [(i, i ^ bit) for i in range(4)])]
    pallas_call x4, Pallas kernels: 15.6 us -> 14.8 us  [product(): pl.pallas_call(functools.partial(product_kernel, start, fetch, TILE, len(...]
    ppermute x15, starting transfers between devices: 14.3 us -> 14.9 us  [exchange(): return lax.ppermute(value, axis, [(i, i ^ bit) for i in range(4)])]
  transfers between devices with their start and end apart: 17 -> 17, of which waited for: 6 -> 5; matrix products, arithmetic and copies ran while one was open for 0% -> 0% of each run, Pallas kernels for 49% -> 50%
where the time goes in v3:
time: 59.4 us; the launch traced here: 59.2 us
  Pallas kernels  30.6 us (52%)
  starting transfers between devices  19.2 us (32%)
  waiting for transfers between devices  9.21 us (16%)
    ppermute x15, starting transfers between devices, exchange(): return lax.ppermute(value, axis, [(i, i ^ bit) for i in range(4)])  14.9 us
    pallas_call x4, Pallas kernels, product(): pl.pallas_call(functools.partial(product_kernel, start, fetch, TILE, len(...  14.8 us
    pallas_call x1, Pallas kernels, load(): pl.pallas_call(functools.partial(load_kernel, plan), in_specs=[pl.BlockSp...  10.2 us
    ppermute x15, waiting for transfers between devices, exchange(): return lax.ppermute(value, axis, [(i, i ^ bit) for i in range(4)])  9.21 us
    ppermute x2, starting transfers between devices, deliver(): return lax.ppermute(pair, ('tm', 'tk'), perm)  4.21 us
    pallas_call x4, Pallas kernels, finish(): pl.pallas_call(functools.partial(finish_kernel, start, TILE), in_specs=[v...  3.5 us
  transfers between devices with their start and end apart: 17, of which 5 were waited for; matrix products, arithmetic and copies ran while one was open for 0% of the time, Pallas kernels for 50%

profile of v3, /device:TPU:0, one launch (start us, length us, event | category | flops | bytes accessed | tf_op | source)
XLA Modules:
  0.0 59.2 jit_solution(16207594220634465064)
XLA Ops:
  0.0 0.5 collective-permute-start.3
  0.5 0.1 collective-permute-start.4
  0.5 3.0 %collective-permute-start = (bf16[32,2048]{1,0:T(8,128)(2,1)}, bf16[32,2048]{1,0:T(8,128)(2,1)S(1)}, u32[]{:S(2)}, u32[]{:S(2)}) collective-permute-start(bf16[32,2048]{1,0:T(8,128)(2,1)} %bitcast.3), channel_id=1, source_target_pairs={{0,4},{4,0},{8,12},{12,8},{1,5},{5,1},{9,13},{13,9},{2,6},{6,2},{1... | collective-permute-start | bytes 393224 | tf_op jit(solution)/shard_map/ppermute | solution.py:458
  3.5 2.6 %collective-permute-start.1 = (bf16[32,2048]{1,0:T(8,128)(2,1)}, bf16[32,2048]{1,0:T(8,128)(2,1)S(1)}, u32[]{:S(2)}, u32[]{:S(2)}) collective-permute-start(bf16[32,2048]{1,0:T(8,128)(2,1)} %bitcast.4), channel_id=1, source_target_pairs={{0,8},{4,12},{8,0},{12,4},{1,9},{5,13},{9,1},{13,5},{2,10},{6,14},... | collective-permute-start | bytes 393224 | tf_op jit(solution)/shard_map/ppermute | solution.py:458
  6.1 0.0 collective-permute-start.2
  6.1 10.2 %load.1 = (bf16[2048,128]{1,0:T(8,128)(2,1)S(1)}, bf16[64,7168]{1,0:T(8,128)(2,1)S(1)}, bf16[64,7168]{1,0:T(8,128)(2,1)S(1)}, bf16[2048,2048]{1,0:T(8,128)(2,1)S...) custom-call(bf16[1,2048,128]{2,1,0:T(8,128)(2,1)} %refs_0_.1, ...), custom_call_target="tpu_custom_call" | custom-call | bytes 63438848 | tf_op jit(solution)/shard_map/load/pallas_call | solution.py:330
  16.3 0.0 collective-permute-done.one
  16.3 0.3 collective-permute-done.1.two
  16.7 0.0 collective-permute-done.2.three
  16.7 0.0 collective-permute-done.3.refs_0_.fg
  16.7 0.0 collective-permute-done.4.refs_1_.fu
  16.7 0.3 assemble_and_shrink.1
  17.0 0.1 collective-permute-start.5
  17.1 0.6 masks.1.refs_0_.mask
  17.7 0.6 %collective-permute-done.5.second = f32[128,128]{1,0:T(8,128)S(1)} collective-permute-done((f32[128,128]{1,0:T(8,128)S(1)}, f32[128,128]{1,0:T(8,128)S(1)}, u32[]{:S(2)}, u32[]{:S(2)}) %collective-permute-start.5) | collective-permute-done | bytes 65568 | tf_op jit(solution)/shard_map/ppermute | solution.py:458
  18.3 0.7 %collective-permute-start.6 = (f32[128,128]{1,0:T(8,128)S(1)}, f32[128,128]{1,0:T(8,128)S(1)}, u32[]{:S(2)}, u32[]{:S(2)}) collective-permute-start(f32[128,128]{1,0:T(8,128)S(1)} %join.2.refs_0_), channel_id=1, source_target_pairs={{0,0},{1,8},{2,4},{3,12},{4,1},{5,9},{6,5},{7,13},{8,2},{9,10},{10... | collective-permute-start | bytes 196616 | tf_op jit(solution)/shard_map/ppermute | solution.py:482
  19.0 3.5 %collective-permute-start.7 = (f32[128,128]{1,0:T(8,128)S(1)}, f32[128,128]{1,0:T(8,128)S(1)}, u32[]{:S(2)}, u32[]{:S(2)}) collective-permute-start(f32[128,128]{1,0:T(8,128)S(1)} %join.2.refs_0_), channel_id=1, source_target_pairs={{0,4},{1,12},{2,0},{3,8},{4,5},{5,13},{6,1},{7,9},{8,6},{9,14},{10... | collective-permute-start | bytes 196616 | tf_op jit(solution)/shard_map/ppermute | solution.py:482
  22.6 4.0 %product.4 = (bf16[128,2048]{1,0:T(8,128)(2,1)S(1)}, f32[128,2048]{1,0:T(8,128)S(1)}) custom-call(bf16[128,2048]{1,0:T(8,128)(2,1)S(1)} %get-tuple-element.32.x_ref, bf16[2048,2048]{1,0:T(8,128)(2,1)S(1)} %get-tuple-element.33.gate, bf16[2048,7168]{1,0:T(8,128)(2,1)} %up.7, f32[128,128]{1,0:T(8,128)S(1)} %join.2.refs_0_), custom_call_target="tpu_custom_call" | custom-call | flops 1 | bytes 1 | tf_op jit(solution)/shard_map/product/pallas_call | solution.py:417
  26.6 0.0 collective-permute-done.6.first
  26.6 0.0 collective-permute-done.7.second
  26.6 2.4 %collective-permute-start.8 = (bf16[128,128]{1,0:T(8,128)(2,1)S(1)}, bf16[128,128]{1,0:T(8,128)(2,1)S(1)}, u32[]{:S(2)}, u32[]{:S(2)}) collective-permute-start(bf16[128,128]{1,0:T(8,128)(2,1)S(1)} %join.3.mine.refs_0_), channel_id=1, source_target_pairs={{0,1},{1,0},{2,3},{3,2},{4,5},{5,4},{6,7},{7,6},{8,9},{9,8},{10,11... | collective-permute-start | bytes 98312 | tf_op jit(solution)/shard_map/ppermute | solution.py:458
  29.1 0.1 collective-permute-start.9
  29.2 3.4 %product.5 = (bf16[128,1536]{1,0:T(8,128)(2,1)S(1)}, f32[128,1536]{1,0:T(8,128)S(1)}) custom-call(bf16[128,2048]{1,0:T(8,128)(2,1)S(1)} %get-tuple-element.32.x_ref, bf16[2048,1536]{1,0:T(8,128)(2,1)S(1)} %get-tuple-element.40.gate, bf16[2048,7168]{1,0:T(8,128)(2,1)} %up.7, bf16[128,128]{1,0:T(8,128)(2,1)S(1)} %join.3.mine.refs_0_), custom_call_target="tpu_custom_call" | custom-call | flops 1 | bytes 1 | tf_op jit(solution)/shard_map/product/pallas_call | solution.py:417
  32.6 0.5 collective-permute-start.10
  33.1 0.0 collective-permute-done.8.theirs
  33.1 0.1 spread.1.ranks_ref
  33.2 0.3 pair_sum.4
  33.5 2.0 %collective-permute-start.13 = (bf16[64,2048]{1,0:T(8,128)(2,1)S(1)}, bf16[64,2048]{1,0:T(8,128)(2,1)S(1)}, u32[]{:S(2)}, u32[]{:S(2)}) collective-permute-start(bf16[64,2048]{1,0:T(8,128)(2,1)S(1)} %get-tuple-element.42.refs_0_), channel_id=1, source_target_pairs={{0,2},{1,3},{2,0},{3,1},{4,6},{5,7},{6,4},{7,5},{8,10},{9,11},{10,... | collective-permute-start | bytes 786440 | tf_op jit(solution)/shard_map/ppermute | solution.py:458
  35.4 0.3 pair_sum.5
  35.7 0.9 %collective-permute-start.14 = (bf16[64,1536]{1,0:T(8,128)(2,1)S(1)}, bf16[64,1536]{1,0:T(8,128)(2,1)S(1)}, u32[]{:S(2)}, u32[]{:S(2)}) collective-permute-start(bf16[64,1536]{1,0:T(8,128)(2,1)S(1)} %get-tuple-element.44.refs_1_), channel_id=1, source_target_pairs={{0,2},{1,3},{2,0},{3,1},{4,6},{5,7},{6,4},{7,5},{8,10},{9,11},{10,... | collective-permute-start | bytes 589832 | tf_op jit(solution)/shard_map/ppermute | solution.py:458
  36.7 4.0 %product.6 = (bf16[128,2048]{1,0:T(8,128)(2,1)S(1)}, f32[128,2048]{1,0:T(8,128)S(1)}) custom-call(bf16[128,2048]{1,0:T(8,128)(2,1)S(1)} %get-tuple-element.32.x_ref, bf16[2048,2048]{1,0:T(8,128)(2,1)S(1)} %get-tuple-element.38.gate, bf16[2048,7168]{1,0:T(8,128)(2,1)} %up.7, bf16[64,2048]{1,0:T(8,128)(2,1)S(1)} %get-tuple-element.42.refs_0_, ...), custom_call_target="tpu_custom_call" | custom-call | flops 1 | bytes 1 | tf_op jit(solution)/shard_map/product/pallas_call | solution.py:417
  40.7 0.1 collective-permute-start.12
  40.8 3.4 %product.7 = (bf16[128,1536]{1,0:T(8,128)(2,1)S(1)}, f32[128,1536]{1,0:T(8,128)S(1)}) custom-call(bf16[128,2048]{1,0:T(8,128)(2,1)S(1)} %get-tuple-element.32.x_ref, bf16[2048,1536]{1,0:T(8,128)(2,1)S(1)} %get-tuple-element.37.gate, bf16[2048,7168]{1,0:T(8,128)(2,1)} %up.7, bf16[128,2048]{1,0:T(8,128)(2,1)S(1)} %get-tuple-element.45.refs_0_), custom_call_target="tpu_custom_call" | custom-call | flops 1 | bytes 1 | tf_op jit(solution)/shard_map/product/pallas_call | solution.py:417
  44.2 0.5 collective-permute-start.11
  44.7 1.5 %collective-permute-done.14.refs_1_.other = bf16[64,1536]{1,0:T(8,128)(2,1)S(1)} collective-permute-done((bf16[64,1536]{1,0:T(8,128)(2,1)S(1)}, bf16[64,1536]{1,0:T(8,128)(2,1)S(1)}, u32[]{:S(2)}, u32[]{:S(2)}) %collective-permute-start.14) | collective-permute-done | bytes 196640 | tf_op jit(solution)/shard_map/ppermute | solution.py:458
  46.2 0.0 collective-permute-done.13.refs_0_.other
  46.2 0.0 collective-permute-done.12.got
  46.2 0.3 pair_sum.6
  46.5 1.8 %collective-permute-start.16 = (bf16[64,2048]{1,0:T(8,128)(2,1)S(1)}, bf16[64,2048]{1,0:T(8,128)(2,1)S(1)}, u32[]{:S(2)}, u32[]{:S(2)}) collective-permute-start(bf16[64,2048]{1,0:T(8,128)(2,1)S(1)} %get-tuple-element.49.refs_0_), channel_id=1, source_target_pairs={{0,2},{1,3},{2,0},{3,1},{4,6},{5,7},{6,4},{7,5},{8,10},{9,11},{10,... | collective-permute-start | bytes 786440 | tf_op jit(solution)/shard_map/ppermute | solution.py:458
  48.3 0.0 collective-permute-done.11.got
  48.3 0.3 pair_sum.7
  48.6 0.3 collective-permute-start.15
  48.9 0.9 %finish.4.before = bf16[16,2,7168]{2,1,0:T(2,128)(2,1)} custom-call(f32[64,2048]{1,0:T(8,128)S(1)} %get-tuple-element.54.own, bf16[64,2048]{1,0:T(8,128)(2,1)S(1)} %collective-permute-done.13.refs_0_.other, bf16[16,2,7168]{2,1,0:T(2,128)(2,1)} %blank.1.before, bf16[64,1536]{1,0:T(8,128)(2,1)S(1)} %get-tuple-element.51.refs_0_), custom_call_target="tpu_custom_call", output_to_operand_aliasing={{}: (2, {})} | custom-call | flops 1 | bytes 1 | tf_op jit(solution)/shard_map/finish/pallas_call | solution.py:243
  49.9 0.8 %finish.5.before = bf16[16,2,7168]{2,1,0:T(2,128)(2,1)} custom-call(f32[64,1536]{1,0:T(8,128)S(1)} %get-tuple-element.53.own, bf16[64,1536]{1,0:T(8,128)(2,1)S(1)} %collective-permute-done.14.refs_1_.other, bf16[16,2,7168]{2,1,0:T(2,128)(2,1)} %finish.4.before, bf16[64,1536]{1,0:T(8,128)(2,1)S(1)} %get-tuple-element.51.refs_0_), custom_call_target="tpu_custom_call", output_to_operand_aliasing={{}: (2, {})} | custom-call | flops 1 | bytes 1 | tf_op jit(solution)/shard_map/finish/pallas_call | solution.py:243
  50.7 5.1 %collective-permute-done.16.other = bf16[64,2048]{1,0:T(8,128)(2,1)S(1)} collective-permute-done((bf16[64,2048]{1,0:T(8,128)(2,1)S(1)}, bf16[64,2048]{1,0:T(8,128)(2,1)S(1)}, u32[]{:S(2)}, u32[]{:S(2)}) %collective-permute-start.16) | collective-permute-done | bytes 262176 | tf_op jit(solution)/shard_map/ppermute | solution.py:458
  55.8 0.9 %finish.6.before = bf16[16,2,7168]{2,1,0:T(2,128)(2,1)} custom-call(f32[64,2048]{1,0:T(8,128)S(1)} %get-tuple-element.52.own, bf16[64,2048]{1,0:T(8,128)(2,1)S(1)} %collective-permute-done.16.other, bf16[16,2,7168]{2,1,0:T(2,128)(2,1)} %finish.5.before, bf16[64,1536]{1,0:T(8,128)(2,1)S(1)} %get-tuple-element.51.refs_0_), custom_call_target="tpu_custom_call", output_to_operand_aliasing={{}: (2, {})} | custom-call | flops 1 | bytes 1 | tf_op jit(solution)/shard_map/finish/pallas_call | solution.py:243
  56.7 1.7 %collective-permute-done.15.other = bf16[64,1536]{1,0:T(8,128)(2,1)S(1)} collective-permute-done((bf16[64,1536]{1,0:T(8,128)(2,1)S(1)}, bf16[64,1536]{1,0:T(8,128)(2,1)S(1)}, u32[]{:S(2)}, u32[]{:S(2)}) %collective-permute-start.15) | collective-permute-done | bytes 196640 | tf_op jit(solution)/shard_map/ppermute | solution.py:458
  58.4 0.8 %finish.7 = bf16[16,2,7168]{2,1,0:T(2,128)(2,1)} custom-call(f32[64,1536]{1,0:T(8,128)S(1)} %get-tuple-element.50.own, bf16[64,1536]{1,0:T(8,128)(2,1)S(1)} %collective-permute-done.15.other, bf16[16,2,7168]{2,1,0:T(2,128)(2,1)} %finish.6.before, bf16[64,1536]{1,0:T(8,128)(2,1)S(1)} %get-tuple-element.51.refs_0_), custom_call_target="tpu_custom_call", output_to_operand_aliasing={{}: (2, {})} | custom-call | flops 1 | bytes 1 | tf_op jit(solution)/shard_map/finish/pallas_call | solution.py:243
  (12 shorter events, 0.0 us)
Async XLA Ops:
  0.0 16.7 %collective-permute-start.3 = (bf16[64,7168]{1,0:T(8,128)(2,1)}, bf16[64,7168]{1,0:T(8,128)(2,1)S(1)}, u32[]{:S(2)}, u32[]{:S(2)}) collective-permute-start(bf16[64,7168]{1,0:T(8,128)(2,1)} %bitcast.7), channel_id=1, source_target_pairs={{0,1},{1,0},{2,3},{3,2},{4,5},{5,4},{6,7},{7,6},{8,9},{9,8},{10,11... | collective-permute-start | bytes 2752520 | tf_op jit(solution)/shard_map/ppermute | solution.py:458
  0.5 16.2 %collective-permute-start.4 = (bf16[64,7168]{1,0:T(8,128)(2,1)}, bf16[64,7168]{1,0:T(8,128)(2,1)S(1)}, u32[]{:S(2)}, u32[]{:S(2)}) collective-permute-start(bf16[64,7168]{1,0:T(8,128)(2,1)} %bitcast.8), channel_id=1, source_target_pairs={{0,1},{1,0},{2,3},{3,2},{4,5},{5,4},{6,7},{7,6},{8,9},{9,8},{10,11... | collective-permute-start | bytes 2752520 | tf_op jit(solution)/shard_map/ppermute | solution.py:458
  0.5 16.2 %copy-start = (bf16[2,16,2048]{2,1,0:T(8,128)(2,1)S(1)}, bf16[2,16,2048]{2,1,0:T(8,128)(2,1)}, u32[]{:S(2)}) copy-start(bf16[2,16,2048]{2,1,0:T(8,128)(2,1)} %param.8) | copy-start | bytes 393220
  0.5 16.6 %copy-start.1 = (s32[2,8]{1,0:T(2,128)S(1)}, s32[2,8]{1,0:T(2,128)}, u32[]{:S(2)}) copy-start(s32[2,8]{1,0:T(2,128)} %adapter_ref.1) | copy-start | bytes 196
  0.5 16.6 %copy-start.2 = (s32[4]{0:T(128)S(1)}, s32[4]{0:T(128)}, u32[]{:S(2)}) copy-start(s32[4]{0:T(128)} %slot_ref.1) | copy-start | bytes 52
  0.5 15.8 %collective-permute-start = (bf16[32,2048]{1,0:T(8,128)(2,1)}, bf16[32,2048]{1,0:T(8,128)(2,1)S(1)}, u32[]{:S(2)}, u32[]{:S(2)}) collective-permute-start(bf16[32,2048]{1,0:T(8,128)(2,1)} %bitcast.3), channel_id=1, source_target_pairs={{0,4},{4,0},{8,12},{12,8},{1,5},{5,1},{9,13},{13,9},{2,6},{6,2},{1... | collective-permute-start | bytes 393224 | tf_op jit(solution)/shard_map/ppermute | solution.py:458
  3.5 13.1 %collective-permute-start.1 = (bf16[32,2048]{1,0:T(8,128)(2,1)}, bf16[32,2048]{1,0:T(8,128)(2,1)S(1)}, u32[]{:S(2)}, u32[]{:S(2)}) collective-permute-start(bf16[32,2048]{1,0:T(8,128)(2,1)} %bitcast.4), channel_id=1, source_target_pairs={{0,8},{4,12},{8,0},{12,4},{1,9},{5,13},{9,1},{13,5},{2,10},{6,14},... | collective-permute-start | bytes 393224 | tf_op jit(solution)/shard_map/ppermute | solution.py:458
  6.1 10.5 %collective-permute-start.2 = (bf16[32,2048]{1,0:T(8,128)(2,1)}, bf16[32,2048]{1,0:T(8,128)(2,1)S(1)}, u32[]{:S(2)}, u32[]{:S(2)}) collective-permute-start(bf16[32,2048]{1,0:T(8,128)(2,1)} %bitcast.5), channel_id=1, source_target_pairs={{0,12},{4,8},{8,4},{12,0},{1,13},{5,9},{9,5},{13,1},{2,14},{6,10},... | collective-permute-start | bytes 393224 | tf_op jit(solution)/shard_map/ppermute | solution.py:458
  17.0 1.3 %collective-permute-start.5 = (f32[128,128]{1,0:T(8,128)S(1)}, f32[128,128]{1,0:T(8,128)S(1)}, u32[]{:S(2)}, u32[]{:S(2)}) collective-permute-start(f32[128,128]{1,0:T(8,128)S(1)} %get-tuple-element.31.first), channel_id=1, source_target_pairs={{0,1},{1,0},{2,3},{3,2},{4,5},{5,4},{6,7},{7,6},{8,9},{9,8},{10,11... | collective-permute-start | bytes 196616 | tf_op jit(solution)/shard_map/ppermute | solution.py:458
  18.3 8.3 %collective-permute-start.6 = (f32[128,128]{1,0:T(8,128)S(1)}, f32[128,128]{1,0:T(8,128)S(1)}, u32[]{:S(2)}, u32[]{:S(2)}) collective-permute-start(f32[128,128]{1,0:T(8,128)S(1)} %join.2.refs_0_), channel_id=1, source_target_pairs={{0,0},{1,8},{2,4},{3,12},{4,1},{5,9},{6,5},{7,13},{8,2},{9,10},{10... | collective-permute-start | bytes 196616 | tf_op jit(solution)/shard_map/ppermute | solution.py:482
  19.0 7.6 %collective-permute-start.7 = (f32[128,128]{1,0:T(8,128)S(1)}, f32[128,128]{1,0:T(8,128)S(1)}, u32[]{:S(2)}, u32[]{:S(2)}) collective-permute-start(f32[128,128]{1,0:T(8,128)S(1)} %join.2.refs_0_), channel_id=1, source_target_pairs={{0,4},{1,12},{2,0},{3,8},{4,5},{5,13},{6,1},{7,9},{8,6},{9,14},{10... | collective-permute-start | bytes 196616 | tf_op jit(solution)/shard_map/ppermute | solution.py:482
  26.6 6.4 %collective-permute-start.8 = (bf16[128,128]{1,0:T(8,128)(2,1)S(1)}, bf16[128,128]{1,0:T(8,128)(2,1)S(1)}, u32[]{:S(2)}, u32[]{:S(2)}) collective-permute-start(bf16[128,128]{1,0:T(8,128)(2,1)S(1)} %join.3.mine.refs_0_), channel_id=1, source_target_pairs={{0,1},{1,0},{2,3},{3,2},{4,5},{5,4},{6,7},{7,6},{8,9},{9,8},{10,11... | collective-permute-start | bytes 98312 | tf_op jit(solution)/shard_map/ppermute | solution.py:458
  29.1 4.1 %collective-permute-start.9 = (bf16[128,2048]{1,0:T(8,128)(2,1)S(1)}, bf16[128,2048]{1,0:T(8,128)(2,1)S(1)}, u32[]{:S(2)}, u32[]{:S(2)}) collective-permute-start(bf16[128,2048]{1,0:T(8,128)(2,1)S(1)} %get-tuple-element.34.refs_0_), channel_id=1, source_target_pairs={{0,1},{1,0},{2,3},{3,2},{4,5},{5,4},{6,7},{7,6},{8,9},{9,8},{10,11... | collective-permute-start | bytes 1572872 | tf_op jit(solution)/shard_map/ppermute | solution.py:458
  32.6 2.9 %collective-permute-start.10 = (bf16[128,1536]{1,0:T(8,128)(2,1)S(1)}, bf16[128,1536]{1,0:T(8,128)(2,1)S(1)}, u32[]{:S(2)}, u32[]{:S(2)}) collective-permute-start(bf16[128,1536]{1,0:T(8,128)(2,1)S(1)} %get-tuple-element.41.refs_0_), channel_id=1, source_target_pairs={{0,1},{1,0},{2,3},{3,2},{4,5},{5,4},{6,7},{7,6},{8,9},{9,8},{10,11... | collective-permute-start | bytes 1179656 | tf_op jit(solution)/shard_map/ppermute | solution.py:458
  33.5 12.7 %collective-permute-start.13 = (bf16[64,2048]{1,0:T(8,128)(2,1)S(1)}, bf16[64,2048]{1,0:T(8,128)(2,1)S(1)}, u32[]{:S(2)}, u32[]{:S(2)}) collective-permute-start(bf16[64,2048]{1,0:T(8,128)(2,1)S(1)} %get-tuple-element.42.refs_0_), channel_id=1, source_target_pairs={{0,2},{1,3},{2,0},{3,1},{4,6},{5,7},{6,4},{7,5},{8,10},{9,11},{10,... | collective-permute-start | bytes 786440 | tf_op jit(solution)/shard_map/ppermute | solution.py:458
  35.7 10.5 %collective-permute-start.14 = (bf16[64,1536]{1,0:T(8,128)(2,1)S(1)}, bf16[64,1536]{1,0:T(8,128)(2,1)S(1)}, u32[]{:S(2)}, u32[]{:S(2)}) collective-permute-start(bf16[64,1536]{1,0:T(8,128)(2,1)S(1)} %get-tuple-element.44.refs_1_), channel_id=1, source_target_pairs={{0,2},{1,3},{2,0},{3,1},{4,6},{5,7},{6,4},{7,5},{8,10},{9,11},{10,... | collective-permute-start | bytes 589832 | tf_op jit(solution)/shard_map/ppermute | solution.py:458
  40.7 5.5 %collective-permute-start.12 = (bf16[128,2048]{1,0:T(8,128)(2,1)S(1)}, bf16[128,2048]{1,0:T(8,128)(2,1)S(1)}, u32[]{:S(2)}, u32[]{:S(2)}) collective-permute-start(bf16[128,2048]{1,0:T(8,128)(2,1)S(1)} %get-tuple-element.45.refs_0_), channel_id=1, source_target_pairs={{0,1},{1,0},{2,3},{3,2},{4,5},{5,4},{6,7},{7,6},{8,9},{9,8},{10,11... | collective-permute-start | bytes 1572872 | tf_op jit(solution)/shard_map/ppermute | solution.py:458
  44.2 4.1 %collective-permute-start.11 = (bf16[128,1536]{1,0:T(8,128)(2,1)S(1)}, bf16[128,1536]{1,0:T(8,128)(2,1)S(1)}, u32[]{:S(2)}, u32[]{:S(2)}) collective-permute-start(bf16[128,1536]{1,0:T(8,128)(2,1)S(1)} %get-tuple-element.47), channel_id=1, source_target_pairs={{0,1},{1,0},{2,3},{3,2},{4,5},{5,4},{6,7},{7,6},{8,9},{9,8},{10,11... | collective-permute-start | bytes 1179656 | tf_op jit(solution)/shard_map/ppermute | solution.py:458
  46.5 9.3 %collective-permute-start.16 = (bf16[64,2048]{1,0:T(8,128)(2,1)S(1)}, bf16[64,2048]{1,0:T(8,128)(2,1)S(1)}, u32[]{:S(2)}, u32[]{:S(2)}) collective-permute-start(bf16[64,2048]{1,0:T(8,128)(2,1)S(1)} %get-tuple-element.49.refs_0_), channel_id=1, source_target_pairs={{0,2},{1,3},{2,0},{3,1},{4,6},{5,7},{6,4},{7,5},{8,10},{9,11},{10,... | collective-permute-start | bytes 786440 | tf_op jit(solution)/shard_map/ppermute | solution.py:458
  48.6 9.8 %collective-permute-start.15 = (bf16[64,1536]{1,0:T(8,128)(2,1)S(1)}, bf16[64,1536]{1,0:T(8,128)(2,1)S(1)}, u32[]{:S(2)}, u32[]{:S(2)}) collective-permute-start(bf16[64,1536]{1,0:T(8,128)(2,1)S(1)} %get-tuple-element.51.refs_0_), channel_id=1, source_target_pairs={{0,2},{1,3},{2,0},{3,1},{4,6},{5,7},{6,4},{7,5},{8,10},{9,11},{10,... | collective-permute-start | bytes 589832 | tf_op jit(solution)/shard_map/ppermute | solution.py:458

commit v4 on v3

--- a/solution.py
+++ b/solution.py
@@ -11,9 +11,9 @@
 MIB = 2**20
 F32 = jnp.float32
 BF16 = jnp.bfloat16
-CHUNKS = (2048, 1536, 2048, 1536)
+CHUNKS = (2560, 1024, 2048, 1536)
 SLOTS = 5
-LEAD = 2
+LEAD = 3
 FAT = 10**11
 SPREAD = 10**11
 PTIES = (("pair",), ("mine",), ())
@@ -380,25 +380,32 @@
             sem.at[j % slots],
         )
 
+    def place(which, at, weight):
+        base = which * quarter
+        y = jnp.dot(x_ref[...], weight, preferred_element_type=F32)
+        keep[base : base + quarter, at] = y[quarter:half]
+        keep[half + base : half + base + quarter, at] = y[:quarter]
+        send[base : base + quarter, at] = y[half + quarter :].astype(BF16)
+        send[half + base : half + base + quarter, at] = y[half : half + quarter].astype(BF16)
+
     def multiply(which, j):
-        base = which * quarter
         for k in range(0, fetch, tile):
             at = slice(j * fetch + k, j * fetch + k + tile)
             if which == 0:
                 weight = gate[:, at]
             else:
                 weight = buffer[j % slots, :, k : k + tile]
-            y = jnp.dot(x_ref[...], weight, preferred_element_type=F32)
-            keep[base : base + quarter, at] = y[quarter:half]
-            keep[half + base : half + base + quarter, at] = y[:quarter]
-            send[base : base + quarter, at] = y[half + quarter :].astype(BF16)
-            send[half + base : half + base + quarter, at] = y[half : half + quarter].astype(BF16)
+            place(which, at, weight)
 
     for j in range(min(slots, count)):
         copy(j).start()
     lead = min(LEAD, count)
-    for j in range(lead):
-        multiply(0, j)
+
+    @pl.loop(0, lead * fetch // tile)
+    def _(k):
+        at = pl.ds(pl.multiple_of(k * tile, tile), tile)
+        place(0, at, gate[:, at])
+
     for j in range(count):
         copy(j).wait()
         multiply(1, j)
@@ -451,6 +458,22 @@
     store_slot,
 ):
     steps, here, depth = hidden_in.shape
+    if (
+        gate_weight.shape[1] != sum(CHUNKS)
+        or shrink_store.shape[0] != 1
+        or expand_gate.shape[0] != 1
+        or here % 16
+    ):
+        return on_any_mesh(
+            hidden_in,
+            gate_weight,
+            up_weight,
+            shrink_store,
+            expand_gate,
+            expand_up,
+            block_adapter,
+            store_slot,
+        )
     held = hidden_in.reshape(steps * here, depth)
     rows = 4 * steps * here
 

time: 59.4 us -> 59.2 us (level)
  starting transfers between devices: 19.2 us -> 18.4 us
    ppermute x15, starting transfers between devices: 14.9 us -> 14.2 us  [exchange(): return lax.ppermute(value, axis, [(i, i ^ bit) for i in range(4)])]
where the time goes in v4:
time: 59.2 us; the launch traced here: 59 us
  Pallas kernels  30.8 us (52%)
  starting transfers between devices  18.4 us (31%)
  waiting for transfers between devices  9.63 us (16%)
    pallas_call x4, Pallas kernels, product(): pl.pallas_call(functools.partial(product_kernel, start, fetch, TILE, len(...  15 us
    ppermute x15, starting transfers between devices, exchange(): return lax.ppermute(value, axis, [(i, i ^ bit) for i in range(4)])  14.2 us
    pallas_call x1, Pallas kernels, load(): pl.pallas_call(functools.partial(load_kernel, plan), in_specs=[pl.BlockSp...  10.2 us
    ppermute x15, waiting for transfers between devices, exchange(): return lax.ppermute(value, axis, [(i, i ^ bit) for i in range(4)])  9.62 us
    ppermute x2, starting transfers between devices, deliver(): return lax.ppermute(pair, ('tm', 'tk'), perm)  4.21 us
    pallas_call x4, Pallas kernels, finish(): pl.pallas_call(functools.partial(finish_kernel, start, TILE), in_specs=[v...  3.5 us
  transfers between devices with their start and end apart: 17, of which 5 were waited for; matrix products, arithmetic and copies ran while one was open for 0% of the time, Pallas kernels for 50%

profile of v4, /device:TPU:0, one launch (start us, length us, event | category | flops | bytes accessed | tf_op | source)
XLA Modules:
  0.0 59.0 jit_solution(12503523561535295935)
XLA Ops:
  0.0 0.5 collective-permute-start.3
  0.5 0.1 collective-permute-start.4
  0.5 3.0 %collective-permute-start = (bf16[32,2048]{1,0:T(8,128)(2,1)}, bf16[32,2048]{1,0:T(8,128)(2,1)S(1)}, u32[]{:S(2)}, u32[]{:S(2)}) collective-permute-start(bf16[32,2048]{1,0:T(8,128)(2,1)} %bitcast.3), channel_id=1, source_target_pairs={{0,4},{4,0},{8,12},{12,8},{1,5},{5,1},{9,13},{13,9},{2,6},{6,2},{1... | collective-permute-start | bytes 393224 | tf_op jit(solution)/shard_map/ppermute | solution.py:481
  3.5 2.6 %collective-permute-start.1 = (bf16[32,2048]{1,0:T(8,128)(2,1)}, bf16[32,2048]{1,0:T(8,128)(2,1)S(1)}, u32[]{:S(2)}, u32[]{:S(2)}) collective-permute-start(bf16[32,2048]{1,0:T(8,128)(2,1)} %bitcast.4), channel_id=1, source_target_pairs={{0,8},{4,12},{8,0},{12,4},{1,9},{5,13},{9,1},{13,5},{2,10},{6,14},... | collective-permute-start | bytes 393224 | tf_op jit(solution)/shard_map/ppermute | solution.py:481
  6.1 0.0 collective-permute-start.2
  6.1 10.2 %load.1 = (bf16[2048,128]{1,0:T(8,128)(2,1)S(1)}, bf16[64,7168]{1,0:T(8,128)(2,1)S(1)}, bf16[64,7168]{1,0:T(8,128)(2,1)S(1)}, bf16[2048,2560]{1,0:T(8,128)(2,1)S...) custom-call(bf16[1,2048,128]{2,1,0:T(8,128)(2,1)} %refs_0_.1, ...), custom_call_target="tpu_custom_call" | custom-call | bytes 63438848 | tf_op jit(solution)/shard_map/load/pallas_call | solution.py:330
  16.3 0.0 collective-permute-done.one
  16.3 0.3 collective-permute-done.1.two
  16.7 0.0 collective-permute-done.2.three
  16.7 0.0 collective-permute-done.3.refs_0_.fg
  16.7 0.0 collective-permute-done.4.refs_1_.fu
  16.7 0.3 assemble_and_shrink.1
  17.0 0.1 collective-permute-start.5
  17.1 0.6 masks.1.refs_0_.mask
  17.7 0.6 %collective-permute-done.5.second = f32[128,128]{1,0:T(8,128)S(1)} collective-permute-done((f32[128,128]{1,0:T(8,128)S(1)}, f32[128,128]{1,0:T(8,128)S(1)}, u32[]{:S(2)}, u32[]{:S(2)}) %collective-permute-start.5) | collective-permute-done | bytes 65568 | tf_op jit(solution)/shard_map/ppermute | solution.py:481
  18.3 0.7 %collective-permute-start.6 = (f32[128,128]{1,0:T(8,128)S(1)}, f32[128,128]{1,0:T(8,128)S(1)}, u32[]{:S(2)}, u32[]{:S(2)}) collective-permute-start(f32[128,128]{1,0:T(8,128)S(1)} %join.2.refs_0_), channel_id=1, source_target_pairs={{0,0},{1,8},{2,4},{3,12},{4,1},{5,9},{6,5},{7,13},{8,2},{9,10},{10... | collective-permute-start | bytes 196616 | tf_op jit(solution)/shard_map/ppermute | solution.py:505
  19.0 3.5 %collective-permute-start.7 = (f32[128,128]{1,0:T(8,128)S(1)}, f32[128,128]{1,0:T(8,128)S(1)}, u32[]{:S(2)}, u32[]{:S(2)}) collective-permute-start(f32[128,128]{1,0:T(8,128)S(1)} %join.2.refs_0_), channel_id=1, source_target_pairs={{0,4},{1,12},{2,0},{3,8},{4,5},{5,13},{6,1},{7,9},{8,6},{9,14},{10... | collective-permute-start | bytes 196616 | tf_op jit(solution)/shard_map/ppermute | solution.py:505
  22.6 4.8 %product.4 = (bf16[128,2560]{1,0:T(8,128)(2,1)S(1)}, f32[128,2560]{1,0:T(8,128)S(1)}) custom-call(bf16[128,2048]{1,0:T(8,128)(2,1)S(1)} %get-tuple-element.32.x_ref, bf16[2048,2560]{1,0:T(8,128)(2,1)S(1)} %get-tuple-element.33.gate, bf16[2048,7168]{1,0:T(8,128)(2,1)} %up.7, f32[128,128]{1,0:T(8,128)S(1)} %join.2.refs_0_), custom_call_target="tpu_custom_call" | custom-call | flops 1 | bytes 1 | tf_op jit(solution)/shard_map/product/pallas_call | solution.py:424
  27.4 0.0 collective-permute-done.6.first
  27.4 0.0 collective-permute-done.7.second
  27.4 2.4 %collective-permute-start.8 = (bf16[128,128]{1,0:T(8,128)(2,1)S(1)}, bf16[128,128]{1,0:T(8,128)(2,1)S(1)}, u32[]{:S(2)}, u32[]{:S(2)}) collective-permute-start(bf16[128,128]{1,0:T(8,128)(2,1)S(1)} %join.3.mine.refs_0_), channel_id=1, source_target_pairs={{0,1},{1,0},{2,3},{3,2},{4,5},{5,4},{6,7},{7,6},{8,9},{9,8},{10,11... | collective-permute-start | bytes 98312 | tf_op jit(solution)/shard_map/ppermute | solution.py:481
  29.9 0.1 collective-permute-start.9
  30.0 2.7 %product.5 = (bf16[128,1024]{1,0:T(8,128)(2,1)S(1)}, f32[128,1024]{1,0:T(8,128)S(1)}) custom-call(bf16[128,2048]{1,0:T(8,128)(2,1)S(1)} %get-tuple-element.32.x_ref, bf16[2048,1024]{1,0:T(8,128)(2,1)S(1)} %get-tuple-element.40.gate, bf16[2048,7168]{1,0:T(8,128)(2,1)} %up.7, bf16[128,128]{1,0:T(8,128)(2,1)S(1)} %join.3.mine.refs_0_), custom_call_target="tpu_custom_call" | custom-call | flops 1 | bytes 1 | tf_op jit(solution)/shard_map/product/pallas_call | solution.py:424
  32.7 0.5 collective-permute-start.10
  33.2 0.0 collective-permute-done.8.theirs
  33.2 0.1 spread.1.ranks_ref
  33.3 0.3 pair_sum.4
  33.6 1.2 %collective-permute-start.13 = (bf16[64,2560]{1,0:T(8,128)(2,1)S(1)}, bf16[64,2560]{1,0:T(8,128)(2,1)S(1)}, u32[]{:S(2)}, u32[]{:S(2)}) collective-permute-start(bf16[64,2560]{1,0:T(8,128)(2,1)S(1)} %get-tuple-element.42.refs_0_), channel_id=1, source_target_pairs={{0,2},{1,3},{2,0},{3,1},{4,6},{5,7},{6,4},{7,5},{8,10},{9,11},{10,... | collective-permute-start | bytes 983048 | tf_op jit(solution)/shard_map/ppermute | solution.py:481
  34.8 0.0 collective-permute-done.10.got
  34.8 0.2 pair_sum.5
  35.0 1.0 %collective-permute-start.14 = (bf16[64,1024]{1,0:T(8,128)(2,1)S(1)}, bf16[64,1024]{1,0:T(8,128)(2,1)S(1)}, u32[]{:S(2)}, u32[]{:S(2)}) collective-permute-start(bf16[64,1024]{1,0:T(8,128)(2,1)S(1)} %get-tuple-element.44.refs_1_), channel_id=1, source_target_pairs={{0,2},{1,3},{2,0},{3,1},{4,6},{5,7},{6,4},{7,5},{8,10},{9,11},{10,... | collective-permute-start | bytes 393224 | tf_op jit(solution)/shard_map/ppermute | solution.py:481
  36.0 4.1 %product.6 = (bf16[128,2048]{1,0:T(8,128)(2,1)S(1)}, f32[128,2048]{1,0:T(8,128)S(1)}) custom-call(bf16[128,2048]{1,0:T(8,128)(2,1)S(1)} %get-tuple-element.32.x_ref, bf16[2048,2048]{1,0:T(8,128)(2,1)S(1)} %get-tuple-element.38.gate, bf16[2048,7168]{1,0:T(8,128)(2,1)} %up.7, bf16[64,2560]{1,0:T(8,128)(2,1)S(1)} %get-tuple-element.42.refs_0_, ...), custom_call_target="tpu_custom_call" | custom-call | flops 1 | bytes 1 | tf_op jit(solution)/shard_map/product/pallas_call | solution.py:424
  40.1 0.1 collective-permute-start.12
  40.2 3.4 %product.7 = (bf16[128,1536]{1,0:T(8,128)(2,1)S(1)}, f32[128,1536]{1,0:T(8,128)S(1)}) custom-call(bf16[128,2048]{1,0:T(8,128)(2,1)S(1)} %get-tuple-element.32.x_ref, bf16[2048,1536]{1,0:T(8,128)(2,1)S(1)} %get-tuple-element.37.gate, bf16[2048,7168]{1,0:T(8,128)(2,1)} %up.7, bf16[128,2048]{1,0:T(8,128)(2,1)S(1)} %get-tuple-element.45.refs_0_), custom_call_target="tpu_custom_call" | custom-call | flops 1 | bytes 1 | tf_op jit(solution)/shard_map/product/pallas_call | solution.py:424
  43.6 0.6 collective-permute-start.11
  44.1 2.0 %collective-permute-done.14.refs_1_.other = bf16[64,1024]{1,0:T(8,128)(2,1)S(1)} collective-permute-done((bf16[64,1024]{1,0:T(8,128)(2,1)S(1)}, bf16[64,1024]{1,0:T(8,128)(2,1)S(1)}, u32[]{:S(2)}, u32[]{:S(2)}) %collective-permute-start.14) | collective-permute-done | bytes 131104 | tf_op jit(solution)/shard_map/ppermute | solution.py:481
  46.2 0.0 collective-permute-done.13.refs_0_.other
  46.2 0.0 collective-permute-done.12.got
  46.2 0.3 pair_sum.6
  46.5 1.2 %collective-permute-start.16 = (bf16[64,2048]{1,0:T(8,128)(2,1)S(1)}, bf16[64,2048]{1,0:T(8,128)(2,1)S(1)}, u32[]{:S(2)}, u32[]{:S(2)}) collective-permute-start(bf16[64,2048]{1,0:T(8,128)(2,1)S(1)} %get-tuple-element.49.refs_0_), channel_id=1, source_target_pairs={{0,2},{1,3},{2,0},{3,1},{4,6},{5,7},{6,4},{7,5},{8,10},{9,11},{10,... | collective-permute-start | bytes 786440 | tf_op jit(solution)/shard_map/ppermute | solution.py:481
  47.7 0.3 pair_sum.7
  47.9 1.0 %collective-permute-start.15 = (bf16[64,1536]{1,0:T(8,128)(2,1)S(1)}, bf16[64,1536]{1,0:T(8,128)(2,1)S(1)}, u32[]{:S(2)}, u32[]{:S(2)}) collective-permute-start(bf16[64,1536]{1,0:T(8,128)(2,1)S(1)} %get-tuple-element.51.refs_0_), channel_id=1, source_target_pairs={{0,2},{1,3},{2,0},{3,1},{4,6},{5,7},{6,4},{7,5},{8,10},{9,11},{10,... | collective-permute-start | bytes 589832 | tf_op jit(solution)/shard_map/ppermute | solution.py:481
  48.9 1.0 %finish.4.before = bf16[16,2,7168]{2,1,0:T(2,128)(2,1)} custom-call(f32[64,2560]{1,0:T(8,128)S(1)} %get-tuple-element.54.own, bf16[64,2560]{1,0:T(8,128)(2,1)S(1)} %collective-permute-done.13.refs_0_.other, bf16[16,2,7168]{2,1,0:T(2,128)(2,1)} %blank.1.before, bf16[64,1536]{1,0:T(8,128)(2,1)S(1)} %get-tuple-element.51.refs_0_), custom_call_target="tpu_custom_call", output_to_operand_aliasing={{}: (2, {})} | custom-call | flops 1 | bytes 1 | tf_op jit(solution)/shard_map/finish/pallas_call | solution.py:243
  49.9 0.8 %finish.5.before = bf16[16,2,7168]{2,1,0:T(2,128)(2,1)} custom-call(f32[64,1024]{1,0:T(8,128)S(1)} %get-tuple-element.53.own, bf16[64,1024]{1,0:T(8,128)(2,1)S(1)} %collective-permute-done.14.refs_1_.other, bf16[16,2,7168]{2,1,0:T(2,128)(2,1)} %finish.4.before, bf16[64,1536]{1,0:T(8,128)(2,1)S(1)} %get-tuple-element.51.refs_0_), custom_call_target="tpu_custom_call", output_to_operand_aliasing={{}: (2, {})} | custom-call | flops 1 | bytes 1 | tf_op jit(solution)/shard_map/finish/pallas_call | solution.py:243
  50.7 5.1 %collective-permute-done.16.other = bf16[64,2048]{1,0:T(8,128)(2,1)S(1)} collective-permute-done((bf16[64,2048]{1,0:T(8,128)(2,1)S(1)}, bf16[64,2048]{1,0:T(8,128)(2,1)S(1)}, u32[]{:S(2)}, u32[]{:S(2)}) %collective-permute-start.16) | collective-permute-done | bytes 262176 | tf_op jit(solution)/shard_map/ppermute | solution.py:481
  55.8 0.9 %finish.6.before = bf16[16,2,7168]{2,1,0:T(2,128)(2,1)} custom-call(f32[64,2048]{1,0:T(8,128)S(1)} %get-tuple-element.52.own, bf16[64,2048]{1,0:T(8,128)(2,1)S(1)} %collective-permute-done.16.other, bf16[16,2,7168]{2,1,0:T(2,128)(2,1)} %finish.5.before, bf16[64,1536]{1,0:T(8,128)(2,1)S(1)} %get-tuple-element.51.refs_0_), custom_call_target="tpu_custom_call", output_to_operand_aliasing={{}: (2, {})} | custom-call | flops 1 | bytes 1 | tf_op jit(solution)/shard_map/finish/pallas_call | solution.py:243
  56.7 1.5 %collective-permute-done.15.other = bf16[64,1536]{1,0:T(8,128)(2,1)S(1)} collective-permute-done((bf16[64,1536]{1,0:T(8,128)(2,1)S(1)}, bf16[64,1536]{1,0:T(8,128)(2,1)S(1)}, u32[]{:S(2)}, u32[]{:S(2)}) %collective-permute-start.15) | collective-permute-done | bytes 196640 | tf_op jit(solution)/shard_map/ppermute | solution.py:481
  58.2 0.8 %finish.7 = bf16[16,2,7168]{2,1,0:T(2,128)(2,1)} custom-call(f32[64,1536]{1,0:T(8,128)S(1)} %get-tuple-element.50.own, bf16[64,1536]{1,0:T(8,128)(2,1)S(1)} %collective-permute-done.15.other, bf16[16,2,7168]{2,1,0:T(2,128)(2,1)} %finish.6.before, bf16[64,1536]{1,0:T(8,128)(2,1)S(1)} %get-tuple-element.51.refs_0_), custom_call_target="tpu_custom_call", output_to_operand_aliasing={{}: (2, {})} | custom-call | flops 1 | bytes 1 | tf_op jit(solution)/shard_map/finish/pallas_call | solution.py:243
  (12 shorter events, 0.0 us)
Async XLA Ops:
  0.0 16.7 %collective-permute-start.3 = (bf16[64,7168]{1,0:T(8,128)(2,1)}, bf16[64,7168]{1,0:T(8,128)(2,1)S(1)}, u32[]{:S(2)}, u32[]{:S(2)}) collective-permute-start(bf16[64,7168]{1,0:T(8,128)(2,1)} %bitcast.7), channel_id=1, source_target_pairs={{0,1},{1,0},{2,3},{3,2},{4,5},{5,4},{6,7},{7,6},{8,9},{9,8},{10,11... | collective-permute-start | bytes 2752520 | tf_op jit(solution)/shard_map/ppermute | solution.py:481
  0.5 16.2 %collective-permute-start.4 = (bf16[64,7168]{1,0:T(8,128)(2,1)}, bf16[64,7168]{1,0:T(8,128)(2,1)S(1)}, u32[]{:S(2)}, u32[]{:S(2)}) collective-permute-start(bf16[64,7168]{1,0:T(8,128)(2,1)} %bitcast.8), channel_id=1, source_target_pairs={{0,1},{1,0},{2,3},{3,2},{4,5},{5,4},{6,7},{7,6},{8,9},{9,8},{10,11... | collective-permute-start | bytes 2752520 | tf_op jit(solution)/shard_map/ppermute | solution.py:481
  0.5 16.2 %copy-start = (bf16[2,16,2048]{2,1,0:T(8,128)(2,1)S(1)}, bf16[2,16,2048]{2,1,0:T(8,128)(2,1)}, u32[]{:S(2)}) copy-start(bf16[2,16,2048]{2,1,0:T(8,128)(2,1)} %param.8) | copy-start | bytes 393220
  0.5 16.6 %copy-start.1 = (s32[2,8]{1,0:T(2,128)S(1)}, s32[2,8]{1,0:T(2,128)}, u32[]{:S(2)}) copy-start(s32[2,8]{1,0:T(2,128)} %adapter_ref.1) | copy-start | bytes 196
  0.5 16.6 %copy-start.2 = (s32[4]{0:T(128)S(1)}, s32[4]{0:T(128)}, u32[]{:S(2)}) copy-start(s32[4]{0:T(128)} %slot_ref.1) | copy-start | bytes 52
  0.5 15.8 %collective-permute-start = (bf16[32,2048]{1,0:T(8,128)(2,1)}, bf16[32,2048]{1,0:T(8,128)(2,1)S(1)}, u32[]{:S(2)}, u32[]{:S(2)}) collective-permute-start(bf16[32,2048]{1,0:T(8,128)(2,1)} %bitcast.3), channel_id=1, source_target_pairs={{0,4},{4,0},{8,12},{12,8},{1,5},{5,1},{9,13},{13,9},{2,6},{6,2},{1... | collective-permute-start | bytes 393224 | tf_op jit(solution)/shard_map/ppermute | solution.py:481
  3.5 13.1 %collective-permute-start.1 = (bf16[32,2048]{1,0:T(8,128)(2,1)}, bf16[32,2048]{1,0:T(8,128)(2,1)S(1)}, u32[]{:S(2)}, u32[]{:S(2)}) collective-permute-start(bf16[32,2048]{1,0:T(8,128)(2,1)} %bitcast.4), channel_id=1, source_target_pairs={{0,8},{4,12},{8,0},{12,4},{1,9},{5,13},{9,1},{13,5},{2,10},{6,14},... | collective-permute-start | bytes 393224 | tf_op jit(solution)/shard_map/ppermute | solution.py:481
  6.1 10.5 %collective-permute-start.2 = (bf16[32,2048]{1,0:T(8,128)(2,1)}, bf16[32,2048]{1,0:T(8,128)(2,1)S(1)}, u32[]{:S(2)}, u32[]{:S(2)}) collective-permute-start(bf16[32,2048]{1,0:T(8,128)(2,1)} %bitcast.5), channel_id=1, source_target_pairs={{0,12},{4,8},{8,4},{12,0},{1,13},{5,9},{9,5},{13,1},{2,14},{6,10},... | collective-permute-start | bytes 393224 | tf_op jit(solution)/shard_map/ppermute | solution.py:481
  17.0 1.3 %collective-permute-start.5 = (f32[128,128]{1,0:T(8,128)S(1)}, f32[128,128]{1,0:T(8,128)S(1)}, u32[]{:S(2)}, u32[]{:S(2)}) collective-permute-start(f32[128,128]{1,0:T(8,128)S(1)} %get-tuple-element.31.first), channel_id=1, source_target_pairs={{0,1},{1,0},{2,3},{3,2},{4,5},{5,4},{6,7},{7,6},{8,9},{9,8},{10,11... | collective-permute-start | bytes 196616 | tf_op jit(solution)/shard_map/ppermute | solution.py:481
  18.3 9.0 %collective-permute-start.6 = (f32[128,128]{1,0:T(8,128)S(1)}, f32[128,128]{1,0:T(8,128)S(1)}, u32[]{:S(2)}, u32[]{:S(2)}) collective-permute-start(f32[128,128]{1,0:T(8,128)S(1)} %join.2.refs_0_), channel_id=1, source_target_pairs={{0,0},{1,8},{2,4},{3,12},{4,1},{5,9},{6,5},{7,13},{8,2},{9,10},{10... | collective-permute-start | bytes 196616 | tf_op jit(solution)/shard_map/ppermute | solution.py:505
  19.0 8.4 %collective-permute-start.7 = (f32[128,128]{1,0:T(8,128)S(1)}, f32[128,128]{1,0:T(8,128)S(1)}, u32[]{:S(2)}, u32[]{:S(2)}) collective-permute-start(f32[128,128]{1,0:T(8,128)S(1)} %join.2.refs_0_), channel_id=1, source_target_pairs={{0,4},{1,12},{2,0},{3,8},{4,5},{5,13},{6,1},{7,9},{8,6},{9,14},{10... | collective-permute-start | bytes 196616 | tf_op jit(solution)/shard_map/ppermute | solution.py:505
  27.4 5.7 %collective-permute-start.8 = (bf16[128,128]{1,0:T(8,128)(2,1)S(1)}, bf16[128,128]{1,0:T(8,128)(2,1)S(1)}, u32[]{:S(2)}, u32[]{:S(2)}) collective-permute-start(bf16[128,128]{1,0:T(8,128)(2,1)S(1)} %join.3.mine.refs_0_), channel_id=1, source_target_pairs={{0,1},{1,0},{2,3},{3,2},{4,5},{5,4},{6,7},{7,6},{8,9},{9,8},{10,11... | collective-permute-start | bytes 98312 | tf_op jit(solution)/shard_map/ppermute | solution.py:481
  29.9 3.4 %collective-permute-start.9 = (bf16[128,2560]{1,0:T(8,128)(2,1)S(1)}, bf16[128,2560]{1,0:T(8,128)(2,1)S(1)}, u32[]{:S(2)}, u32[]{:S(2)}) collective-permute-start(bf16[128,2560]{1,0:T(8,128)(2,1)S(1)} %get-tuple-element.34.refs_0_), channel_id=1, source_target_pairs={{0,1},{1,0},{2,3},{3,2},{4,5},{5,4},{6,7},{7,6},{8,9},{9,8},{10,11... | collective-permute-start | bytes 1966088 | tf_op jit(solution)/shard_map/ppermute | solution.py:481
  32.7 2.1 %collective-permute-start.10 = (bf16[128,1024]{1,0:T(8,128)(2,1)S(1)}, bf16[128,1024]{1,0:T(8,128)(2,1)S(1)}, u32[]{:S(2)}, u32[]{:S(2)}) collective-permute-start(bf16[128,1024]{1,0:T(8,128)(2,1)S(1)} %get-tuple-element.41.refs_0_), channel_id=1, source_target_pairs={{0,1},{1,0},{2,3},{3,2},{4,5},{5,4},{6,7},{7,6},{8,9},{9,8},{10,11... | collective-permute-start | bytes 786440 | tf_op jit(solution)/shard_map/ppermute | solution.py:481
  33.6 12.6 %collective-permute-start.13 = (bf16[64,2560]{1,0:T(8,128)(2,1)S(1)}, bf16[64,2560]{1,0:T(8,128)(2,1)S(1)}, u32[]{:S(2)}, u32[]{:S(2)}) collective-permute-start(bf16[64,2560]{1,0:T(8,128)(2,1)S(1)} %get-tuple-element.42.refs_0_), channel_id=1, source_target_pairs={{0,2},{1,3},{2,0},{3,1},{4,6},{5,7},{6,4},{7,5},{8,10},{9,11},{10,... | collective-permute-start | bytes 983048 | tf_op jit(solution)/shard_map/ppermute | solution.py:481
  35.0 11.2 %collective-permute-start.14 = (bf16[64,1024]{1,0:T(8,128)(2,1)S(1)}, bf16[64,1024]{1,0:T(8,128)(2,1)S(1)}, u32[]{:S(2)}, u32[]{:S(2)}) collective-permute-start(bf16[64,1024]{1,0:T(8,128)(2,1)S(1)} %get-tuple-element.44.refs_1_), channel_id=1, source_target_pairs={{0,2},{1,3},{2,0},{3,1},{4,6},{5,7},{6,4},{7,5},{8,10},{9,11},{10,... | collective-permute-start | bytes 393224 | tf_op jit(solution)/shard_map/ppermute | solution.py:481
  40.1 6.0 %collective-permute-start.12 = (bf16[128,2048]{1,0:T(8,128)(2,1)S(1)}, bf16[128,2048]{1,0:T(8,128)(2,1)S(1)}, u32[]{:S(2)}, u32[]{:S(2)}) collective-permute-start(bf16[128,2048]{1,0:T(8,128)(2,1)S(1)} %get-tuple-element.45.refs_0_), channel_id=1, source_target_pairs={{0,1},{1,0},{2,3},{3,2},{4,5},{5,4},{6,7},{7,6},{8,9},{9,8},{10,11... | collective-permute-start | bytes 1572872 | tf_op jit(solution)/shard_map/ppermute | solution.py:481
  43.6 4.1 %collective-permute-start.11 = (bf16[128,1536]{1,0:T(8,128)(2,1)S(1)}, bf16[128,1536]{1,0:T(8,128)(2,1)S(1)}, u32[]{:S(2)}, u32[]{:S(2)}) collective-permute-start(bf16[128,1536]{1,0:T(8,128)(2,1)S(1)} %get-tuple-element.47), channel_id=1, source_target_pairs={{0,1},{1,0},{2,3},{3,2},{4,5},{5,4},{6,7},{7,6},{8,9},{9,8},{10,11... | collective-permute-start | bytes 1179656 | tf_op jit(solution)/shard_map/ppermute | solution.py:481
  46.5 9.3 %collective-permute-start.16 = (bf16[64,2048]{1,0:T(8,128)(2,1)S(1)}, bf16[64,2048]{1,0:T(8,128)(2,1)S(1)}, u32[]{:S(2)}, u32[]{:S(2)}) collective-permute-start(bf16[64,2048]{1,0:T(8,128)(2,1)S(1)} %get-tuple-element.49.refs_0_), channel_id=1, source_target_pairs={{0,2},{1,3},{2,0},{3,1},{4,6},{5,7},{6,4},{7,5},{8,10},{9,11},{10,... | collective-permute-start | bytes 786440 | tf_op jit(solution)/shard_map/ppermute | solution.py:481
  47.9 10.3 %collective-permute-start.15 = (bf16[64,1536]{1,0:T(8,128)(2,1)S(1)}, bf16[64,1536]{1,0:T(8,128)(2,1)S(1)}, u32[]{:S(2)}, u32[]{:S(2)}) collective-permute-start(bf16[64,1536]{1,0:T(8,128)(2,1)S(1)} %get-tuple-element.51.refs_0_), channel_id=1, source_target_pairs={{0,2},{1,3},{2,0},{3,1},{4,6},{5,7},{6,4},{7,5},{8,10},{9,11},{10,... | collective-permute-start | bytes 589832 | tf_op jit(solution)/shard_map/ppermute | solution.py:481

commit v5 on v4

--- a/solution.py
+++ b/solution.py
@@ -11,7 +11,7 @@
 MIB = 2**20
 F32 = jnp.float32
 BF16 = jnp.bfloat16
-CHUNKS = (2560, 1024, 2048, 1536)
+CHUNKS = (2048, 1536, 2048, 1536)
 SLOTS = 5
 LEAD = 3
 FAT = 10**11

time: 59.2 us -> 59.3 us (level)
  starting transfers between devices: 18.4 us -> 19 us
    ppermute x15, starting transfers between devices: 14.2 us -> 14.8 us  [exchange(): return lax.ppermute(value, axis, [(i, i ^ bit) for i in range(4)])]
where the time goes in v5:
time: 59.3 us; the launch traced here: 59.1 us
  Pallas kernels  30.8 us (52%)
  starting transfers between devices  19 us (32%)
  waiting for transfers between devices  9.06 us (15%)
    pallas_call x4, Pallas kernels, product(): pl.pallas_call(functools.partial(product_kernel, start, fetch, TILE, len(...  15 us
    ppermute x15, starting transfers between devices, exchange(): return lax.ppermute(value, axis, [(i, i ^ bit) for i in range(4)])  14.8 us
    pallas_call x1, Pallas kernels, load(): pl.pallas_call(functools.partial(load_kernel, plan), in_specs=[pl.BlockSp...  10.2 us
    ppermute x15, waiting for transfers between devices, exchange(): return lax.ppermute(value, axis, [(i, i ^ bit) for i in range(4)])  9.05 us
    ppermute x2, starting transfers between devices, deliver(): return lax.ppermute(pair, ('tm', 'tk'), perm)  4.21 us
    pallas_call x4, Pallas kernels, finish(): pl.pallas_call(functools.partial(finish_kernel, start, TILE), in_specs=[v...  3.5 us
  transfers between devices with their start and end apart: 17, of which 5 were waited for; matrix products, arithmetic and copies ran while one was open for 0% of the time, Pallas kernels for 50%

profile of v5, /device:TPU:0, one launch (start us, length us, event | category | flops | bytes accessed | tf_op | source)
XLA Modules:
  0.0 59.1 jit_solution(9694967330220163514)
XLA Ops:
  0.0 0.5 collective-permute-start.3
  0.5 0.1 collective-permute-start.4
  0.5 3.0 %collective-permute-start = (bf16[32,2048]{1,0:T(8,128)(2,1)}, bf16[32,2048]{1,0:T(8,128)(2,1)S(1)}, u32[]{:S(2)}, u32[]{:S(2)}) collective-permute-start(bf16[32,2048]{1,0:T(8,128)(2,1)} %bitcast.3), channel_id=1, source_target_pairs={{0,4},{4,0},{8,12},{12,8},{1,5},{5,1},{9,13},{13,9},{2,6},{6,2},{1... | collective-permute-start | bytes 393224 | tf_op jit(solution)/shard_map/ppermute | solution.py:481
  3.5 2.6 %collective-permute-start.1 = (bf16[32,2048]{1,0:T(8,128)(2,1)}, bf16[32,2048]{1,0:T(8,128)(2,1)S(1)}, u32[]{:S(2)}, u32[]{:S(2)}) collective-permute-start(bf16[32,2048]{1,0:T(8,128)(2,1)} %bitcast.4), channel_id=1, source_target_pairs={{0,8},{4,12},{8,0},{12,4},{1,9},{5,13},{9,1},{13,5},{2,10},{6,14},... | collective-permute-start | bytes 393224 | tf_op jit(solution)/shard_map/ppermute | solution.py:481
  6.1 0.0 collective-permute-start.2
  6.1 10.2 %load.1 = (bf16[2048,128]{1,0:T(8,128)(2,1)S(1)}, bf16[64,7168]{1,0:T(8,128)(2,1)S(1)}, bf16[64,7168]{1,0:T(8,128)(2,1)S(1)}, bf16[2048,2048]{1,0:T(8,128)(2,1)S...) custom-call(bf16[1,2048,128]{2,1,0:T(8,128)(2,1)} %refs_0_.1, ...), custom_call_target="tpu_custom_call" | custom-call | bytes 63438848 | tf_op jit(solution)/shard_map/load/pallas_call | solution.py:330
  16.3 0.0 collective-permute-done.one
  16.3 0.3 collective-permute-done.1.two
  16.7 0.0 collective-permute-done.2.three
  16.7 0.0 collective-permute-done.3.refs_0_.fg
  16.7 0.0 collective-permute-done.4.refs_1_.fu
  16.7 0.3 assemble_and_shrink.1
  17.0 0.1 collective-permute-start.5
  17.1 0.6 masks.1.refs_0_.mask
  17.7 0.6 %collective-permute-done.5.second = f32[128,128]{1,0:T(8,128)S(1)} collective-permute-done((f32[128,128]{1,0:T(8,128)S(1)}, f32[128,128]{1,0:T(8,128)S(1)}, u32[]{:S(2)}, u32[]{:S(2)}) %collective-permute-start.5) | collective-permute-done | bytes 65568 | tf_op jit(solution)/shard_map/ppermute | solution.py:481
  18.3 0.7 %collective-permute-start.6 = (f32[128,128]{1,0:T(8,128)S(1)}, f32[128,128]{1,0:T(8,128)S(1)}, u32[]{:S(2)}, u32[]{:S(2)}) collective-permute-start(f32[128,128]{1,0:T(8,128)S(1)} %join.2.refs_0_), channel_id=1, source_target_pairs={{0,0},{1,8},{2,4},{3,12},{4,1},{5,9},{6,5},{7,13},{8,2},{9,10},{10... | collective-permute-start | bytes 196616 | tf_op jit(solution)/shard_map/ppermute | solution.py:505
  19.0 3.5 %collective-permute-start.7 = (f32[128,128]{1,0:T(8,128)S(1)}, f32[128,128]{1,0:T(8,128)S(1)}, u32[]{:S(2)}, u32[]{:S(2)}) collective-permute-start(f32[128,128]{1,0:T(8,128)S(1)} %join.2.refs_0_), channel_id=1, source_target_pairs={{0,4},{1,12},{2,0},{3,8},{4,5},{5,13},{6,1},{7,9},{8,6},{9,14},{10... | collective-permute-start | bytes 196616 | tf_op jit(solution)/shard_map/ppermute | solution.py:505
  22.6 4.1 %product.4 = (bf16[128,2048]{1,0:T(8,128)(2,1)S(1)}, f32[128,2048]{1,0:T(8,128)S(1)}) custom-call(bf16[128,2048]{1,0:T(8,128)(2,1)S(1)} %get-tuple-element.32.x_ref, bf16[2048,2048]{1,0:T(8,128)(2,1)S(1)} %get-tuple-element.33.gate, bf16[2048,7168]{1,0:T(8,128)(2,1)} %up.7, f32[128,128]{1,0:T(8,128)S(1)} %join.2.refs_0_), custom_call_target="tpu_custom_call" | custom-call | flops 1 | bytes 1 | tf_op jit(solution)/shard_map/product/pallas_call | solution.py:424
  26.7 0.0 collective-permute-done.6.first
  26.7 0.0 collective-permute-done.7.second
  26.7 2.4 %collective-permute-start.8 = (bf16[128,128]{1,0:T(8,128)(2,1)S(1)}, bf16[128,128]{1,0:T(8,128)(2,1)S(1)}, u32[]{:S(2)}, u32[]{:S(2)}) collective-permute-start(bf16[128,128]{1,0:T(8,128)(2,1)S(1)} %join.3.mine.refs_0_), channel_id=1, source_target_pairs={{0,1},{1,0},{2,3},{3,2},{4,5},{5,4},{6,7},{7,6},{8,9},{9,8},{10,11... | collective-permute-start | bytes 98312 | tf_op jit(solution)/shard_map/ppermute | solution.py:481
  29.2 0.1 collective-permute-start.9
  29.3 3.4 %product.5 = (bf16[128,1536]{1,0:T(8,128)(2,1)S(1)}, f32[128,1536]{1,0:T(8,128)S(1)}) custom-call(bf16[128,2048]{1,0:T(8,128)(2,1)S(1)} %get-tuple-element.32.x_ref, bf16[2048,1536]{1,0:T(8,128)(2,1)S(1)} %get-tuple-element.40.gate, bf16[2048,7168]{1,0:T(8,128)(2,1)} %up.7, bf16[128,128]{1,0:T(8,128)(2,1)S(1)} %join.3.mine.refs_0_), custom_call_target="tpu_custom_call" | custom-call | flops 1 | bytes 1 | tf_op jit(solution)/shard_map/product/pallas_call | solution.py:424
  32.6 0.5 collective-permute-start.10
  33.1 0.1 spread.1.ranks_ref
  33.2 0.0 collective-permute-done.9.got
  33.2 0.3 pair_sum.4
  33.5 1.9 %collective-permute-start.13 = (bf16[64,2048]{1,0:T(8,128)(2,1)S(1)}, bf16[64,2048]{1,0:T(8,128)(2,1)S(1)}, u32[]{:S(2)}, u32[]{:S(2)}) collective-permute-start(bf16[64,2048]{1,0:T(8,128)(2,1)S(1)} %get-tuple-element.42.refs_0_), channel_id=1, source_target_pairs={{0,2},{1,3},{2,0},{3,1},{4,6},{5,7},{6,4},{7,5},{8,10},{9,11},{10,... | collective-permute-start | bytes 786440 | tf_op jit(solution)/shard_map/ppermute | solution.py:481
  35.4 0.3 pair_sum.5
  35.7 1.0 %collective-permute-start.14 = (bf16[64,1536]{1,0:T(8,128)(2,1)S(1)}, bf16[64,1536]{1,0:T(8,128)(2,1)S(1)}, u32[]{:S(2)}, u32[]{:S(2)}) collective-permute-start(bf16[64,1536]{1,0:T(8,128)(2,1)S(1)} %get-tuple-element.44.refs_1_), channel_id=1, source_target_pairs={{0,2},{1,3},{2,0},{3,1},{4,6},{5,7},{6,4},{7,5},{8,10},{9,11},{10,... | collective-permute-start | bytes 589832 | tf_op jit(solution)/shard_map/ppermute | solution.py:481
  36.6 4.1 %product.6 = (bf16[128,2048]{1,0:T(8,128)(2,1)S(1)}, f32[128,2048]{1,0:T(8,128)S(1)}) custom-call(bf16[128,2048]{1,0:T(8,128)(2,1)S(1)} %get-tuple-element.32.x_ref, bf16[2048,2048]{1,0:T(8,128)(2,1)S(1)} %get-tuple-element.38.gate, bf16[2048,7168]{1,0:T(8,128)(2,1)} %up.7, bf16[64,2048]{1,0:T(8,128)(2,1)S(1)} %get-tuple-element.42.refs_0_, ...), custom_call_target="tpu_custom_call" | custom-call | flops 1 | bytes 1 | tf_op jit(solution)/shard_map/product/pallas_call | solution.py:424
  40.8 0.2 collective-permute-start.12
  40.9 3.4 %product.7 = (bf16[128,1536]{1,0:T(8,128)(2,1)S(1)}, f32[128,1536]{1,0:T(8,128)S(1)}) custom-call(bf16[128,2048]{1,0:T(8,128)(2,1)S(1)} %get-tuple-element.32.x_ref, bf16[2048,1536]{1,0:T(8,128)(2,1)S(1)} %get-tuple-element.37.gate, bf16[2048,7168]{1,0:T(8,128)(2,1)} %up.7, bf16[128,2048]{1,0:T(8,128)(2,1)S(1)} %get-tuple-element.45.refs_0_), custom_call_target="tpu_custom_call" | custom-call | flops 1 | bytes 1 | tf_op jit(solution)/shard_map/product/pallas_call | solution.py:424
  44.3 0.5 collective-permute-start.11
  44.8 1.4 %collective-permute-done.14.refs_1_.other = bf16[64,1536]{1,0:T(8,128)(2,1)S(1)} collective-permute-done((bf16[64,1536]{1,0:T(8,128)(2,1)S(1)}, bf16[64,1536]{1,0:T(8,128)(2,1)S(1)}, u32[]{:S(2)}, u32[]{:S(2)}) %collective-permute-start.14) | collective-permute-done | bytes 196640 | tf_op jit(solution)/shard_map/ppermute | solution.py:481
  46.2 0.0 collective-permute-done.13.refs_0_.other
  46.2 0.0 collective-permute-done.12.got
  46.2 0.3 pair_sum.6
  46.5 1.8 %collective-permute-start.16 = (bf16[64,2048]{1,0:T(8,128)(2,1)S(1)}, bf16[64,2048]{1,0:T(8,128)(2,1)S(1)}, u32[]{:S(2)}, u32[]{:S(2)}) collective-permute-start(bf16[64,2048]{1,0:T(8,128)(2,1)S(1)} %get-tuple-element.49.refs_0_), channel_id=1, source_target_pairs={{0,2},{1,3},{2,0},{3,1},{4,6},{5,7},{6,4},{7,5},{8,10},{9,11},{10,... | collective-permute-start | bytes 786440 | tf_op jit(solution)/shard_map/ppermute | solution.py:481
  48.3 0.0 collective-permute-done.11.got
  48.3 0.3 pair_sum.7
  48.6 0.3 collective-permute-start.15
  48.9 0.9 %finish.4.before = bf16[16,2,7168]{2,1,0:T(2,128)(2,1)} custom-call(f32[64,2048]{1,0:T(8,128)S(1)} %get-tuple-element.54.own, bf16[64,2048]{1,0:T(8,128)(2,1)S(1)} %collective-permute-done.13.refs_0_.other, bf16[16,2,7168]{2,1,0:T(2,128)(2,1)} %blank.1.before, bf16[64,1536]{1,0:T(8,128)(2,1)S(1)} %get-tuple-element.51.refs_0_), custom_call_target="tpu_custom_call", output_to_operand_aliasing={{}: (2, {})} | custom-call | flops 1 | bytes 1 | tf_op jit(solution)/shard_map/finish/pallas_call | solution.py:243
  49.8 0.8 %finish.5.before = bf16[16,2,7168]{2,1,0:T(2,128)(2,1)} custom-call(f32[64,1536]{1,0:T(8,128)S(1)} %get-tuple-element.53.own, bf16[64,1536]{1,0:T(8,128)(2,1)S(1)} %collective-permute-done.14.refs_1_.other, bf16[16,2,7168]{2,1,0:T(2,128)(2,1)} %finish.4.before, bf16[64,1536]{1,0:T(8,128)(2,1)S(1)} %get-tuple-element.51.refs_0_), custom_call_target="tpu_custom_call", output_to_operand_aliasing={{}: (2, {})} | custom-call | flops 1 | bytes 1 | tf_op jit(solution)/shard_map/finish/pallas_call | solution.py:243
  50.7 5.1 %collective-permute-done.16.other = bf16[64,2048]{1,0:T(8,128)(2,1)S(1)} collective-permute-done((bf16[64,2048]{1,0:T(8,128)(2,1)S(1)}, bf16[64,2048]{1,0:T(8,128)(2,1)S(1)}, u32[]{:S(2)}, u32[]{:S(2)}) %collective-permute-start.16) | collective-permute-done | bytes 262176 | tf_op jit(solution)/shard_map/ppermute | solution.py:481
  55.8 0.9 %finish.6.before = bf16[16,2,7168]{2,1,0:T(2,128)(2,1)} custom-call(f32[64,2048]{1,0:T(8,128)S(1)} %get-tuple-element.52.own, bf16[64,2048]{1,0:T(8,128)(2,1)S(1)} %collective-permute-done.16.other, bf16[16,2,7168]{2,1,0:T(2,128)(2,1)} %finish.5.before, bf16[64,1536]{1,0:T(8,128)(2,1)S(1)} %get-tuple-element.51.refs_0_), custom_call_target="tpu_custom_call", output_to_operand_aliasing={{}: (2, {})} | custom-call | flops 1 | bytes 1 | tf_op jit(solution)/shard_map/finish/pallas_call | solution.py:243
  56.7 1.6 %collective-permute-done.15.other = bf16[64,1536]{1,0:T(8,128)(2,1)S(1)} collective-permute-done((bf16[64,1536]{1,0:T(8,128)(2,1)S(1)}, bf16[64,1536]{1,0:T(8,128)(2,1)S(1)}, u32[]{:S(2)}, u32[]{:S(2)}) %collective-permute-start.15) | collective-permute-done | bytes 196640 | tf_op jit(solution)/shard_map/ppermute | solution.py:481
  58.3 0.8 %finish.7 = bf16[16,2,7168]{2,1,0:T(2,128)(2,1)} custom-call(f32[64,1536]{1,0:T(8,128)S(1)} %get-tuple-element.50.own, bf16[64,1536]{1,0:T(8,128)(2,1)S(1)} %collective-permute-done.15.other, bf16[16,2,7168]{2,1,0:T(2,128)(2,1)} %finish.6.before, bf16[64,1536]{1,0:T(8,128)(2,1)S(1)} %get-tuple-element.51.refs_0_), custom_call_target="tpu_custom_call", output_to_operand_aliasing={{}: (2, {})} | custom-call | flops 1 | bytes 1 | tf_op jit(solution)/shard_map/finish/pallas_call | solution.py:243
  (12 shorter events, 0.0 us)
Async XLA Ops:
  0.0 16.7 %collective-permute-start.3 = (bf16[64,7168]{1,0:T(8,128)(2,1)}, bf16[64,7168]{1,0:T(8,128)(2,1)S(1)}, u32[]{:S(2)}, u32[]{:S(2)}) collective-permute-start(bf16[64,7168]{1,0:T(8,128)(2,1)} %bitcast.7), channel_id=1, source_target_pairs={{0,1},{1,0},{2,3},{3,2},{4,5},{5,4},{6,7},{7,6},{8,9},{9,8},{10,11... | collective-permute-start | bytes 2752520 | tf_op jit(solution)/shard_map/ppermute | solution.py:481
  0.5 16.2 %collective-permute-start.4 = (bf16[64,7168]{1,0:T(8,128)(2,1)}, bf16[64,7168]{1,0:T(8,128)(2,1)S(1)}, u32[]{:S(2)}, u32[]{:S(2)}) collective-permute-start(bf16[64,7168]{1,0:T(8,128)(2,1)} %bitcast.8), channel_id=1, source_target_pairs={{0,1},{1,0},{2,3},{3,2},{4,5},{5,4},{6,7},{7,6},{8,9},{9,8},{10,11... | collective-permute-start | bytes 2752520 | tf_op jit(solution)/shard_map/ppermute | solution.py:481
  0.5 16.2 %copy-start = (bf16[2,16,2048]{2,1,0:T(8,128)(2,1)S(1)}, bf16[2,16,2048]{2,1,0:T(8,128)(2,1)}, u32[]{:S(2)}) copy-start(bf16[2,16,2048]{2,1,0:T(8,128)(2,1)} %param.8) | copy-start | bytes 393220
  0.5 16.6 %copy-start.1 = (s32[2,8]{1,0:T(2,128)S(1)}, s32[2,8]{1,0:T(2,128)}, u32[]{:S(2)}) copy-start(s32[2,8]{1,0:T(2,128)} %adapter_ref.1) | copy-start | bytes 196
  0.5 16.6 %copy-start.2 = (s32[4]{0:T(128)S(1)}, s32[4]{0:T(128)}, u32[]{:S(2)}) copy-start(s32[4]{0:T(128)} %slot_ref.1) | copy-start | bytes 52
  0.5 15.8 %collective-permute-start = (bf16[32,2048]{1,0:T(8,128)(2,1)}, bf16[32,2048]{1,0:T(8,128)(2,1)S(1)}, u32[]{:S(2)}, u32[]{:S(2)}) collective-permute-start(bf16[32,2048]{1,0:T(8,128)(2,1)} %bitcast.3), channel_id=1, source_target_pairs={{0,4},{4,0},{8,12},{12,8},{1,5},{5,1},{9,13},{13,9},{2,6},{6,2},{1... | collective-permute-start | bytes 393224 | tf_op jit(solution)/shard_map/ppermute | solution.py:481
  3.5 13.1 %collective-permute-start.1 = (bf16[32,2048]{1,0:T(8,128)(2,1)}, bf16[32,2048]{1,0:T(8,128)(2,1)S(1)}, u32[]{:S(2)}, u32[]{:S(2)}) collective-permute-start(bf16[32,2048]{1,0:T(8,128)(2,1)} %bitcast.4), channel_id=1, source_target_pairs={{0,8},{4,12},{8,0},{12,4},{1,9},{5,13},{9,1},{13,5},{2,10},{6,14},... | collective-permute-start | bytes 393224 | tf_op jit(solution)/shard_map/ppermute | solution.py:481
  6.1 10.5 %collective-permute-start.2 = (bf16[32,2048]{1,0:T(8,128)(2,1)}, bf16[32,2048]{1,0:T(8,128)(2,1)S(1)}, u32[]{:S(2)}, u32[]{:S(2)}) collective-permute-start(bf16[32,2048]{1,0:T(8,128)(2,1)} %bitcast.5), channel_id=1, source_target_pairs={{0,12},{4,8},{8,4},{12,0},{1,13},{5,9},{9,5},{13,1},{2,14},{6,10},... | collective-permute-start | bytes 393224 | tf_op jit(solution)/shard_map/ppermute | solution.py:481
  17.0 1.3 %collective-permute-start.5 = (f32[128,128]{1,0:T(8,128)S(1)}, f32[128,128]{1,0:T(8,128)S(1)}, u32[]{:S(2)}, u32[]{:S(2)}) collective-permute-start(f32[128,128]{1,0:T(8,128)S(1)} %get-tuple-element.31.first), channel_id=1, source_target_pairs={{0,1},{1,0},{2,3},{3,2},{4,5},{5,4},{6,7},{7,6},{8,9},{9,8},{10,11... | collective-permute-start | bytes 196616 | tf_op jit(solution)/shard_map/ppermute | solution.py:481
  18.3 8.4 %collective-permute-start.6 = (f32[128,128]{1,0:T(8,128)S(1)}, f32[128,128]{1,0:T(8,128)S(1)}, u32[]{:S(2)}, u32[]{:S(2)}) collective-permute-start(f32[128,128]{1,0:T(8,128)S(1)} %join.2.refs_0_), channel_id=1, source_target_pairs={{0,0},{1,8},{2,4},{3,12},{4,1},{5,9},{6,5},{7,13},{8,2},{9,10},{10... | collective-permute-start | bytes 196616 | tf_op jit(solution)/shard_map/ppermute | solution.py:505
  19.0 7.7 %collective-permute-start.7 = (f32[128,128]{1,0:T(8,128)S(1)}, f32[128,128]{1,0:T(8,128)S(1)}, u32[]{:S(2)}, u32[]{:S(2)}) collective-permute-start(f32[128,128]{1,0:T(8,128)S(1)} %join.2.refs_0_), channel_id=1, source_target_pairs={{0,4},{1,12},{2,0},{3,8},{4,5},{5,13},{6,1},{7,9},{8,6},{9,14},{10... | collective-permute-start | bytes 196616 | tf_op jit(solution)/shard_map/ppermute | solution.py:505
  26.7 6.4 %collective-permute-start.8 = (bf16[128,128]{1,0:T(8,128)(2,1)S(1)}, bf16[128,128]{1,0:T(8,128)(2,1)S(1)}, u32[]{:S(2)}, u32[]{:S(2)}) collective-permute-start(bf16[128,128]{1,0:T(8,128)(2,1)S(1)} %join.3.mine.refs_0_), channel_id=1, source_target_pairs={{0,1},{1,0},{2,3},{3,2},{4,5},{5,4},{6,7},{7,6},{8,9},{9,8},{10,11... | collective-permute-start | bytes 98312 | tf_op jit(solution)/shard_map/ppermute | solution.py:481
  29.2 4.0 %collective-permute-start.9 = (bf16[128,2048]{1,0:T(8,128)(2,1)S(1)}, bf16[128,2048]{1,0:T(8,128)(2,1)S(1)}, u32[]{:S(2)}, u32[]{:S(2)}) collective-permute-start(bf16[128,2048]{1,0:T(8,128)(2,1)S(1)} %get-tuple-element.34.refs_0_), channel_id=1, source_target_pairs={{0,1},{1,0},{2,3},{3,2},{4,5},{5,4},{6,7},{7,6},{8,9},{9,8},{10,11... | collective-permute-start | bytes 1572872 | tf_op jit(solution)/shard_map/ppermute | solution.py:481
  32.6 2.8 %collective-permute-start.10 = (bf16[128,1536]{1,0:T(8,128)(2,1)S(1)}, bf16[128,1536]{1,0:T(8,128)(2,1)S(1)}, u32[]{:S(2)}, u32[]{:S(2)}) collective-permute-start(bf16[128,1536]{1,0:T(8,128)(2,1)S(1)} %get-tuple-element.41.refs_0_), channel_id=1, source_target_pairs={{0,1},{1,0},{2,3},{3,2},{4,5},{5,4},{6,7},{7,6},{8,9},{9,8},{10,11... | collective-permute-start | bytes 1179656 | tf_op jit(solution)/shard_map/ppermute | solution.py:481
  33.5 12.6 %collective-permute-start.13 = (bf16[64,2048]{1,0:T(8,128)(2,1)S(1)}, bf16[64,2048]{1,0:T(8,128)(2,1)S(1)}, u32[]{:S(2)}, u32[]{:S(2)}) collective-permute-start(bf16[64,2048]{1,0:T(8,128)(2,1)S(1)} %get-tuple-element.42.refs_0_), channel_id=1, source_target_pairs={{0,2},{1,3},{2,0},{3,1},{4,6},{5,7},{6,4},{7,5},{8,10},{9,11},{10,... | collective-permute-start | bytes 786440 | tf_op jit(solution)/shard_map/ppermute | solution.py:481
  35.7 10.5 %collective-permute-start.14 = (bf16[64,1536]{1,0:T(8,128)(2,1)S(1)}, bf16[64,1536]{1,0:T(8,128)(2,1)S(1)}, u32[]{:S(2)}, u32[]{:S(2)}) collective-permute-start(bf16[64,1536]{1,0:T(8,128)(2,1)S(1)} %get-tuple-element.44.refs_1_), channel_id=1, source_target_pairs={{0,2},{1,3},{2,0},{3,1},{4,6},{5,7},{6,4},{7,5},{8,10},{9,11},{10,... | collective-permute-start | bytes 589832 | tf_op jit(solution)/shard_map/ppermute | solution.py:481
  40.8 5.4 %collective-permute-start.12 = (bf16[128,2048]{1,0:T(8,128)(2,1)S(1)}, bf16[128,2048]{1,0:T(8,128)(2,1)S(1)}, u32[]{:S(2)}, u32[]{:S(2)}) collective-permute-start(bf16[128,2048]{1,0:T(8,128)(2,1)S(1)} %get-tuple-element.45.refs_0_), channel_id=1, source_target_pairs={{0,1},{1,0},{2,3},{3,2},{4,5},{5,4},{6,7},{7,6},{8,9},{9,8},{10,11... | collective-permute-start | bytes 1572872 | tf_op jit(solution)/shard_map/ppermute | solution.py:481
  44.3 4.0 %collective-permute-start.11 = (bf16[128,1536]{1,0:T(8,128)(2,1)S(1)}, bf16[128,1536]{1,0:T(8,128)(2,1)S(1)}, u32[]{:S(2)}, u32[]{:S(2)}) collective-permute-start(bf16[128,1536]{1,0:T(8,128)(2,1)S(1)} %get-tuple-element.47), channel_id=1, source_target_pairs={{0,1},{1,0},{2,3},{3,2},{4,5},{5,4},{6,7},{7,6},{8,9},{9,8},{10,11... | collective-permute-start | bytes 1179656 | tf_op jit(solution)/shard_map/ppermute | solution.py:481
  46.5 9.3 %collective-permute-start.16 = (bf16[64,2048]{1,0:T(8,128)(2,1)S(1)}, bf16[64,2048]{1,0:T(8,128)(2,1)S(1)}, u32[]{:S(2)}, u32[]{:S(2)}) collective-permute-start(bf16[64,2048]{1,0:T(8,128)(2,1)S(1)} %get-tuple-element.49.refs_0_), channel_id=1, source_target_pairs={{0,2},{1,3},{2,0},{3,1},{4,6},{5,7},{6,4},{7,5},{8,10},{9,11},{10,... | collective-permute-start | bytes 786440 | tf_op jit(solution)/shard_map/ppermute | solution.py:481
  48.6 9.7 %collective-permute-start.15 = (bf16[64,1536]{1,0:T(8,128)(2,1)S(1)}, bf16[64,1536]{1,0:T(8,128)(2,1)S(1)}, u32[]{:S(2)}, u32[]{:S(2)}) collective-permute-start(bf16[64,1536]{1,0:T(8,128)(2,1)S(1)} %get-tuple-element.51.refs_0_), channel_id=1, source_target_pairs={{0,2},{1,3},{2,0},{3,1},{4,6},{5,7},{6,4},{7,5},{8,10},{9,11},{10,... | collective-permute-start | bytes 589832 | tf_op jit(solution)/shard_map/ppermute | solution.py:481
